TPU v7x, 32 devices: a whole 2x2x4 slice. The times are simulated.
32 devices in a mesh: ctx: 16 (over z, y, x), head: 2 (over core).
Axes of the slice: x: 2, y: 2, z: 4, core: 2. Of those that a mesh axis runs over, the one named last changes fastest.
Arguments:
- space_head_input: bfloat16 [8192, 6144], P('ctx', 'head'), may hold values from -6 to 6
- mixer_gate_input: bfloat16 [8192, 6144], P('ctx', 'head'), may hold values from -12 to 12
- state_write_matrix: bfloat16 [8192, 128], P('ctx'), may hold values from -1.78125 to 1.78125
- readout_matrix: bfloat16 [8192, 128], P('ctx'), may hold values from -1.78125 to 1.78125
- head_decay_code: int32 [24], P('head'), may hold values from 0 to 7
- token_step_code: int32 [24, 8192], P('head', 'ctx'), may hold values from 0 to 3
- forget_token_code: int32 [8192], P('ctx'), may hold values from 0 to 3, as said below
- head_direct_gain: float32 [24], P('head'), may hold values from 0.5 to 1.5
- output_norm_gain: float32 [6144], P('head'), may hold values from 0.5 to 1.5
- attention_query: bfloat16 [8192, 3072], P('ctx', 'head'), may hold values from -6.5 to 6.5
- attention_key: bfloat16 [8192, 3072], P('ctx', 'head'), may hold values from -6.5 to 6.5
- attention_value: bfloat16 [8192, 3072], P('ctx', 'head'), may hold values from -6 to 6
Outputs:
- mixer_out: bfloat16 [8192, 6144], P('ctx', 'head')
- window_out: bfloat16 [8192, 3072], P('ctx', 'head')
Inputs may be any that keep to these rules, and one draw needn't show every extreme that they name: `forget_token_code`: at most four tokens have a nonzero code; one has 3.
All inputs are finite; a program needn't handle non-finite values.
Results may differ from a plain program's by a relative error of at most 0.0043.
Values may be sent and summed in bfloat16 or wider, within the bound.
A program may use at most 256 MiB of HBM per device.

v0:
```python
import math

import jax
import jax.numpy as jnp
from jax import lax
from jax.sharding import PartitionSpec as P

HD = 128
SSM_HEADS = 24
P_SIZE = 256
WINDOW = 2048
BLOCK = 256


def passed_along(value, axis, steps):
    count = lax.axis_size(axis)
    initial, last = (max(0, -steps), min(count, count - steps))
    return lax.ppermute(value, axis, [(source, source + steps) for source in range(initial, last)])


def carried_in(value, axis, join, neutral):
    count, mine = (lax.axis_size(axis), lax.axis_index(axis))
    pieces = jax.tree.map(lambda part: lax.all_gather(part, axis), value)
    running = jax.tree.map(
        lambda part, zero: jnp.full_like(part, 0) + jnp.asarray(zero, part.dtype), value, neutral
    )

    def turn(position, running):
        longer = join(running, jax.tree.map(lambda part: part[position], pieces))
        return jax.tree.map(lambda new, old: jnp.where(position < mine, new, old), longer, running)

    return lax.fori_loop(0, count - 1, turn, running)


def head_rates(head_decay_code, token_total_count):
    level_count = head_decay_code.astype(jnp.float32)
    quick_log = math.log(0.03) - level_count / 4.0 * math.log(0.03 * token_total_count)
    gentle = -math.log(token_total_count) - (level_count - 4.0) / 3.0 * math.log(4.0)
    return jnp.exp(jnp.where(level_count <= 4.0, quick_log, gentle))


def decay_factors(head_decay_code, token_step_code, forget_token_code, token_total_count):
    every_rate = head_rates(head_decay_code, token_total_count)
    token_step_sizes = jnp.sqrt(2.0 * every_rate)[:, None] * jnp.exp(
        math.log(2.0) * (0.5 * token_step_code.astype(jnp.float32) - 0.75)
    )
    logarithm_decay = (
        -jnp.sqrt(0.5 * every_rate)[:, None] * token_step_sizes
        - 0.2 * forget_token_code.astype(jnp.float32)[None, :]
    )
    return (token_step_sizes, logarithm_decay)


def join_states(earlier, later_part):
    return (earlier[0] * later_part[0], later_part[0][:, None, None] * earlier[1] + later_part[1])


def per_device(
    space_head_input,
    mixer_gate_input,
    state_write_matrix,
    readout_matrix,
    head_decay_code,
    token_step_code,
    forget_token_code,
    head_direct_gain,
    output_norm_gain,
    attention_query,
    attention_key,
    attention_value,
):
    highest = lax.Precision.HIGHEST
    sequence_length = space_head_input.shape[0]
    local_heads = head_decay_code.shape[0]
    head_width = space_head_input.shape[1] // local_heads
    device_list = lax.axis_size("ctx")
    position = lax.axis_index("ctx")
    reach_back = (WINDOW + sequence_length - 2) // sequence_length
    pair_local = (attention_key, attention_value)
    earlier_blocks = []
    for hop_index in range(1, reach_back + 1):
        earlier_blocks.append(passed_along((pair_local[0], pair_local[1]), "ctx", hop_index))
    token_step_sizes, logarithm_decay = decay_factors(
        head_decay_code, token_step_code, forget_token_code, sequence_length * device_list
    )
    blocks = sequence_length // BLOCK
    inputs_block = space_head_input.reshape(blocks, BLOCK, local_heads, head_width)
    write_block = state_write_matrix.reshape(blocks, BLOCK, -1)
    read_block = readout_matrix.reshape(blocks, BLOCK, -1)
    sizes_block = token_step_sizes.reshape(local_heads, blocks, BLOCK)
    cumulative = jnp.cumsum(logarithm_decay.reshape(local_heads, blocks, BLOCK), axis=2)
    tail_weights = jnp.exp(cumulative[:, :, -1:] - cumulative) * sizes_block
    inputs_wide = inputs_block.astype(jnp.float32)
    fresh_state = jnp.einsum(
        "bshp,hbsn->hbpn",
        inputs_wide,
        tail_weights[..., None] * write_block.astype(jnp.float32)[None],
        precision=highest,
    )
    block_decay = jnp.exp(cumulative[:, :, -1])
    running = jnp.zeros_like(fresh_state[:, 0])
    gain_run = jnp.ones((local_heads,), jnp.float32)
    local_starts = []
    start_gains = []
    for block_index in range(blocks):
        local_starts.append(running)
        start_gains.append(gain_run)
        running = block_decay[:, block_index, None, None] * running + fresh_state[:, block_index]
        gain_run = gain_run * block_decay[:, block_index]
    identity = (jnp.ones_like(gain_run), jnp.zeros_like(running))
    _, incoming = carried_in((gain_run, running), "ctx", join_states, identity)
    starts = jnp.stack(
        [
            start_gains[block_index][:, None, None] * incoming + local_starts[block_index]
            for block_index in range(blocks)
        ],
        axis=1,
    )
    lower_mask = jnp.arange(BLOCK)[:, None] >= jnp.arange(BLOCK)[None, :]
    cross_map = jnp.einsum(
        "btn,bsn->bts", read_block, write_block, preferred_element_type=jnp.float32
    )
    gap_matrix = cumulative[:, :, :, None] - cumulative[:, :, None, :]
    mixing = jnp.where(
        lower_mask,
        jnp.exp(jnp.where(lower_mask, gap_matrix, 0.0))
        * cross_map[None]
        * sizes_block[:, :, None, :],
        0.0,
    ).astype(jnp.bfloat16)
    intra_part = jnp.einsum(
        "hbts,bshp->bthp", mixing, inputs_block, preferred_element_type=jnp.float32
    )
    inter_part = (
        jnp.einsum("btn,hbpn->bthp", read_block.astype(jnp.float32), starts, precision=highest)
        * jnp.transpose(jnp.exp(cumulative), (1, 2, 0))[..., None]
    )
    mixed_all = (intra_part + inter_part).reshape(
        sequence_length, local_heads, head_width
    ) + head_direct_gain[None, :, None] * space_head_input.reshape(
        sequence_length, local_heads, head_width
    ).astype(
        jnp.float32
    )
    gated_out = mixed_all.reshape(sequence_length, local_heads * head_width) * jax.nn.silu(
        mixer_gate_input.astype(jnp.float32)
    )
    squares = lax.psum(jnp.sum(gated_out * gated_out, axis=1), "head")
    mixer_out = (
        gated_out * lax.rsqrt(squares[:, None] / (SSM_HEADS * P_SIZE) + 1e-05) * output_norm_gain
    ).astype(jnp.bfloat16)
    ordered = earlier_blocks[::-1]
    key_all = jnp.concatenate([entry[0] for entry in ordered] + [attention_key], axis=0)
    value_all = jnp.concatenate([entry[1] for entry in ordered] + [attention_value], axis=0)
    score_scale = HD ** (-0.5)
    query_rows = min(sequence_length, 512)
    offset_rows = reach_back * sequence_length
    heads_local = attention_query.shape[1] // HD
    key_first = max(0, offset_rows - WINDOW + 1)
    key_stop = offset_rows + query_rows
    query_pos = position * sequence_length + 0 + jnp.arange(query_rows, dtype=jnp.int32)
    key_pos = (
        (position - reach_back) * sequence_length
        + key_first
        + jnp.arange(key_stop - key_first, dtype=jnp.int32)
    )
    in_window = (
        (key_pos[None, :] <= query_pos[:, None])
        & (key_pos[None, :] > query_pos[:, None] - WINDOW)
        & (key_pos[None, :] >= 0)
    )
    head_parts = []
    for head_index in range(heads_local):
        col_first = head_index * HD
        query_head = attention_query[0:query_rows, col_first : col_first + HD]
        key_head = key_all[key_first:key_stop, col_first : col_first + HD]
        value_head = value_all[key_first:key_stop, col_first : col_first + HD]
        scores = (
            jnp.einsum("qd,kd->qk", query_head, key_head, preferred_element_type=jnp.float32)
            * score_scale
        )
        scores = jnp.where(in_window, scores, -jnp.inf)
        maximum = jnp.max(scores, axis=1, keepdims=True)
        weights_f = jnp.exp(scores - maximum)
        row_total = jnp.sum(weights_f, axis=1, keepdims=True)
        attended = (
            jnp.dot(weights_f.astype(jnp.bfloat16), value_head, preferred_element_type=jnp.float32)
            / row_total
        )
        head_parts.append(attended.astype(jnp.bfloat16))
    window_parts = jnp.concatenate(head_parts, axis=1)
    return (mixer_out, window_parts)


def solution(mesh):
    return jax.shard_map(
        per_device,
        mesh=mesh,
        in_specs=(
            P("ctx", "head"),
            P("ctx", "head"),
            P("ctx", None),
            P("ctx", None),
            P("head"),
            P("head", "ctx"),
            P("ctx"),
            P("head"),
            P("head"),
            P("ctx", "head"),
            P("ctx", "head"),
            P("ctx", "head"),
        ),
        out_specs=(P("ctx", "head"), P("ctx", "head")),
        check_vma=False,
    )
```

profile of v0, /device:TPU:9, one launch (start us, length us, event | category | flops | bytes accessed | tf_op | source)
XLA Modules:
  0.0 715.8 jit_solution(3587393004978052233)
XLA Ops:
  15.5 3.5 reshape.177
  24.0 6.7 fusion.83
  38.1 4.1 collective-permute-start.1
  50.8 333.7 %all-reduce = f32[192]{0:T(256)S(1)} all-reduce(f32[192]{0:T(256)} %copy-done.20), channel_id=2, replica_groups=mesh['ctx'=16,'head'=2] {'ctx'}, use_global_device_ids=true, to_apply=%add | all-reduce | flops 192 | bytes 1536
  384.6 4.6 copy.80
  390.2 5.8 fusion.30
  396.0 15.2 %collective-permute-start.5 = (bf16[512,1536]{1,0:T(8,128)(2,1)S(1)}, bf16[512,1536]{1,0:T(8,128)(2,1)S(1)}, u32[]{:S(2)}, u32[]{:S(2)}) collective-permute-start(bf16[512,1536]{1,0:T(8,128)(2,1)S(1)} %copy-done.8), channel_id=1, source_target_pairs={{0,6},{2,8},{4,10},{6,12},{8,14},{10,16},{12,18},{14,20},{16,22},{... | collective-permute-start | bytes 4718600 | tf_op jit(solution)/shard_map/ppermute | solution.py:18
  412.8 5.5 collective-permute-start.6
  427.6 19.2 %collective-permute-done.5 = bf16[512,1536]{1,0:T(8,128)(2,1)S(1)} collective-permute-done((bf16[512,1536]{1,0:T(8,128)(2,1)S(1)}, bf16[512,1536]{1,0:T(8,128)(2,1)S(1)}, u32[]{:S(2)}, u32[]{:S(2)}) %collective-permute-start.5) | collective-permute-done | bytes 1572896 | tf_op jit(solution)/shard_map/ppermute | solution.py:18
  446.9 33.1 %collective-permute-done.6 = bf16[512,1536]{1,0:T(8,128)(2,1)S(1)} collective-permute-done((bf16[512,1536]{1,0:T(8,128)(2,1)S(1)}, bf16[512,1536]{1,0:T(8,128)(2,1)S(1)}, u32[]{:S(2)}, u32[]{:S(2)}) %collective-permute-start.6) | collective-permute-done | bytes 1572896 | tf_op jit(solution)/shard_map/ppermute | solution.py:18
  480.2 63.4 %collective-permute-done.7 = bf16[512,1536]{1,0:T(8,128)(2,1)S(1)} collective-permute-done((bf16[512,1536]{1,0:T(8,128)(2,1)S(1)}, bf16[512,1536]{1,0:T(8,128)(2,1)S(1)}, u32[]{:S(2)}, u32[]{:S(2)}) %collective-permute-start.7) | collective-permute-done | bytes 1572896 | tf_op jit(solution)/shard_map/ppermute | solution.py:18
  546.9 3.6 fusion.243
  571.3 3.4 fusion.249
  575.5 5.1 fusion.250
  587.8 5.1 fusion.252
  592.9 3.3 fusion.24
  602.6 3.4 fusion.254
  635.2 31.2 %while.14 = (s32[]{:T(128)}, f32[12,256,128]{2,1,0:T(8,128)S(1)}, s32[]{:T(128)}, f32[16,12]{1,0:T(8,128)S(1)}, f32[16,12,256,128]{3,2,1,0:T(8,128)}, /*index=5*/s32[]{:T(128)}, s32[]{:T(128)}) while((s32[]{:T(128)}, f32[12,256,128]{2,1,0:T(8,128)S(1)}, s32[]{:T(128)}, f32[16,12]{1,0:T(8,128)S(1)}, f32[16,12,256,128]{3,2,1,0:T(8,128)}, ...), condition=%wide.region_3.4_spmd.clone, body=%wide.region_2.3_spmd.clone.sunk | while | flops 1572868 | bytes 4718841 | solution.py:32
  668.6 7.0 fusion.5
  675.5 10.2 %copy.78 = f32[2,256,12,256]{1,0,3,2:T(2,128)} copy(f32[2,256,12,256]{3,1,2,0:T(8,128)} %fusion.5) | data formatting | bytes 12582912 | tf_op jit(solution)/shard_map/add | solution.py:138
  685.7 3.7 copy.87
  690.4 4.6 multiply_reduce_fusion
  695.0 6.9 psum.7
  701.9 3.5 multiply_convert_fusion
  (196 shorter events, 144.8 us)
Async XLA Ops:
  7.2 382.8 %copy-start = (bf16[512,128]{1,0:T(8,128)(2,1)S(1)}, bf16[512,128]{1,0:T(8,128)(2,1)}, u32[]{:S(2)}) copy-start(bf16[512,128]{1,0:T(8,128)(2,1)} %param.17) | copy-start | bytes 393220
  7.2 628.0 %all-gather.3.cloned.1.call-start = ((), (), s32[]{:S(2)}) async-start(), calls=%async_computation | async-start | bytes 26738688 | tf_op jit(solution)/shard_map/all_gather | solution.py:23
  15.4 15.3 %copy-start.1 = (bf16[512,3072]{0,1:T(8,128)(2,1)}, bf16[512,3072]{0,1:T(8,128)(2,1)S(1)}, u32[]{:S(2)}) copy-start(bf16[512,3072]{0,1:T(8,128)(2,1)S(1)} %copy.65) | copy-start | bytes 9437188
  24.0 9.1 %copy-start.17 = (f32[12]{0:T(128)}, f32[12]{0:T(128)S(1)}, u32[]{:S(2)}) copy-start(f32[12]{0:T(128)S(1)} %get-tuple-element.151) | copy-start | bytes 148
  24.0 9.1 %copy-start.20 = (f32[192]{0:T(256)}, f32[192]{0:T(256)S(1)}, u32[]{:S(2)}) copy-start(f32[192]{0:T(256)S(1)} %get-tuple-element.152) | copy-start | bytes 2308
  30.7 18.8 %copy-start.13 = (f32[12,2,256]{2,1,0:T(2,128)S(1)}, f32[12,2,256]{2,1,0:T(2,128)}, u32[]{:S(2)}) copy-start(f32[12,2,256]{2,1,0:T(2,128)} %copy-done.12) | copy-start | bytes 73732
  30.7 19.5 %copy-start.14 = (f32[12,2,256]{2,1,0:T(2,128)S(1)}, f32[12,2,256]{2,1,0:T(2,128)}, u32[]{:S(2)}) copy-start(f32[12,2,256]{2,1,0:T(2,128)} %mul.307) | copy-start | bytes 73732
  30.7 353.8 %copy-start.15 = (f32[2,256,12]{1,0,2:T(2,128)S(1)}, f32[2,256,12]{1,0,2:T(2,128)}, u32[]{:S(2)}) copy-start(f32[2,256,12]{1,0,2:T(2,128)} %get-tuple-element.148) | copy-start | bytes 73732
  33.1 356.8 %copy-start.9 = (bf16[512,128]{1,0:T(8,128)(2,1)S(1)}, bf16[512,128]{1,0:T(8,128)(2,1)}, u32[]{:S(2)}) copy-start(bf16[512,128]{1,0:T(8,128)(2,1)} %param.16) | copy-start | bytes 393220
  34.9 361.1 %collective-permute-start = (bf16[512,1536]{1,0:T(8,128)(2,1)S(1)}, bf16[512,1536]{1,0:T(8,128)(2,1)}, u32[]{:S(2)}, u32[]{:S(2)}) collective-permute-start(bf16[512,1536]{1,0:T(8,128)(2,1)S(1)} %copy-done.7), channel_id=1, source_target_pairs={{0,8},{2,10},{4,12},{6,14},{8,16},{10,18},{12,20},{14,22},{16,24},... | collective-permute-start | bytes 4718600 | tf_op jit(solution)/shard_map/ppermute | solution.py:18
  38.1 374.7 %collective-permute-start.1 = (bf16[512,1536]{1,0:T(8,128)(2,1)S(1)}, bf16[512,1536]{1,0:T(8,128)(2,1)}, u32[]{:S(2)}, u32[]{:S(2)}) collective-permute-start(bf16[512,1536]{1,0:T(8,128)(2,1)S(1)} %copy-done.7), channel_id=1, source_target_pairs={{0,6},{2,8},{4,10},{6,12},{8,14},{10,16},{12,18},{14,20},{16,22},{... | collective-permute-start | bytes 4718600 | tf_op jit(solution)/shard_map/ppermute | solution.py:18
  42.2 377.6 %collective-permute-start.2 = (bf16[512,1536]{1,0:T(8,128)(2,1)S(1)}, bf16[512,1536]{1,0:T(8,128)(2,1)}, u32[]{:S(2)}, u32[]{:S(2)}) collective-permute-start(bf16[512,1536]{1,0:T(8,128)(2,1)S(1)} %copy-done.7), channel_id=1, source_target_pairs={{0,4},{2,6},{4,8},{6,10},{8,12},{10,14},{12,16},{14,18},{16,20},{1... | collective-permute-start | bytes 4718600 | tf_op jit(solution)/shard_map/ppermute | solution.py:18
  45.3 377.9 %collective-permute-start.3 = (bf16[512,1536]{1,0:T(8,128)(2,1)S(1)}, bf16[512,1536]{1,0:T(8,128)(2,1)}, u32[]{:S(2)}, u32[]{:S(2)}) collective-permute-start(bf16[512,1536]{1,0:T(8,128)(2,1)S(1)} %copy-done.7), channel_id=1, source_target_pairs={{0,2},{2,4},{4,6},{6,8},{8,10},{10,12},{12,14},{14,16},{16,18},{18... | collective-permute-start | bytes 4718600 | tf_op jit(solution)/shard_map/ppermute | solution.py:18
  47.6 377.3 %collective-permute-start.4 = (bf16[512,1536]{1,0:T(8,128)(2,1)}, bf16[512,1536]{1,0:T(8,128)(2,1)}, u32[]{:S(2)}, u32[]{:S(2)}) collective-permute-start(bf16[512,1536]{1,0:T(8,128)(2,1)} %param.25), channel_id=1, source_target_pairs={{0,8},{2,10},{4,12},{6,14},{8,16},{10,18},{12,20},{14,22},{16,24},... | collective-permute-start | bytes 4718600 | tf_op jit(solution)/shard_map/ppermute | solution.py:18
  390.2 5.8 copy-start.8
  396.0 50.8 %collective-permute-start.5 = (bf16[512,1536]{1,0:T(8,128)(2,1)S(1)}, bf16[512,1536]{1,0:T(8,128)(2,1)S(1)}, u32[]{:S(2)}, u32[]{:S(2)}) collective-permute-start(bf16[512,1536]{1,0:T(8,128)(2,1)S(1)} %copy-done.8), channel_id=1, source_target_pairs={{0,6},{2,8},{4,10},{6,12},{8,14},{10,16},{12,18},{14,20},{16,22},{... | collective-permute-start | bytes 4718600 | tf_op jit(solution)/shard_map/ppermute | solution.py:18
  412.8 67.3 %collective-permute-start.6 = (bf16[512,1536]{1,0:T(8,128)(2,1)S(1)}, bf16[512,1536]{1,0:T(8,128)(2,1)S(1)}, u32[]{:S(2)}, u32[]{:S(2)}) collective-permute-start(bf16[512,1536]{1,0:T(8,128)(2,1)S(1)} %copy-done.8), channel_id=1, source_target_pairs={{0,4},{2,6},{4,8},{6,10},{8,12},{10,14},{12,16},{14,18},{16,20},{1... | collective-permute-start | bytes 4718600 | tf_op jit(solution)/shard_map/ppermute | solution.py:18
  419.8 123.7 %collective-permute-start.7 = (bf16[512,1536]{1,0:T(8,128)(2,1)S(1)}, bf16[512,1536]{1,0:T(8,128)(2,1)S(1)}, u32[]{:S(2)}, u32[]{:S(2)}) collective-permute-start(bf16[512,1536]{1,0:T(8,128)(2,1)S(1)} %copy-done.8), channel_id=1, source_target_pairs={{0,2},{2,4},{4,6},{6,8},{8,10},{10,12},{12,14},{14,16},{16,18},{18... | collective-permute-start | bytes 4718600 | tf_op jit(solution)/shard_map/ppermute | solution.py:18
  424.9 118.7 %copy-start.10 = (bf16[2560,1536]{1,0:T(8,128)(2,1)}, bf16[2560,1536]{1,0:T(8,128)(2,1)S(1)}, u32[]{:S(2)}) copy-start(bf16[2560,1536]{1,0:T(8,128)(2,1)S(1)} %constant_dynamic-update-slice_fusion) | copy-start | bytes 23592964
  574.7 5.9 copy-start.4
  587.0 5.9 copy-start.5
  635.2 31.7 %copy-start.18 = (f32[12]{0:T(128)S(1)}, f32[12]{0:T(128)}, u32[]{:S(2)}) copy-start(f32[12]{0:T(128)} %copy-done.17) | copy-start | bytes 148
  635.2 31.7 %copy-start.19 = (f32[12]{0:T(128)S(1)}, f32[12]{0:T(128)}, u32[]{:S(2)}) copy-start(f32[12]{0:T(128)} %get-tuple-element.149) | copy-start | bytes 148
  690.4 11.5 %copy-start.16 = (f32[3072]{0:T(1024)S(1)}, f32[3072]{0:T(1024)}, u32[]{:S(2)}) copy-start(f32[3072]{0:T(1024)} %param.22) | copy-start | bytes 36868
  (16 other events, 53.3 us)
Sparse Core Ops, SparseCore 0:
  35.0 382.9 all-gather.2
where the time goes:
time: 724 us; the launch traced here: 716 us
  blocking collectives  341 us (47%)
  waiting for transfers between devices  116 us (16%)
  matrix products  88.5 us (12%)
  other arithmetic  62.1 us (9%)
  local copies, waits for them, and re-layouts  55.2 us (8%)
  starting transfers between devices  37.3 us (5%)
  between operations  15.9 us (2%)
    unnamed x1, blocking collectives  334 us
    ppermute x8, waiting for transfers between devices, passed_along(): lax.ppermute(value, axis, [(source, source + steps) for source in range(i...  116 us
    dot_general x12, matrix products, per_device(): jnp.einsum('qd,kd->qk', query_head, key_head, preferred_element_type=jnp....  43.1 us
    ppermute x8, starting transfers between devices, passed_along(): lax.ppermute(value, axis, [(source, source + steps) for source in range(i...  37.2 us
    unnamed x77, local copies, waits for them, and re-layouts  34.2 us
    select_n x15, other arithmetic, turn(): jnp.where(position < mine, new, old)  30.5 us
    dot_general x12, matrix products, per_device(): jnp.dot(weights_f.astype(jnp.bfloat16), value_head, preferred_element_typ...  25.7 us
  transfers between devices with their start and end apart: 9, of which 3 were waited for; matrix products, arithmetic and copies ran while one was open for 15% of the time, Pallas kernels for 0%

commit v1 on v0

v1 whole, which is shorter than its diff:
```python
import functools
import math

import jax
import jax.numpy as jnp
from jax import lax
from jax.experimental import pallas as pl
from jax.experimental.pallas import tpu as pltpu
from jax.sharding import PartitionSpec as P

HD = 128
SSM_HEADS = 24
P_SIZE = 256
WINDOW = 2048
HEAD_GROUPS = 2
VMEM_LIMIT = 48 * 1024 * 1024


def head_rates(head_decay_code, token_total_count):
    level_count = head_decay_code.astype(jnp.float32)
    quick_log = math.log(0.03) - level_count / 4.0 * math.log(0.03 * token_total_count)
    gentle = -math.log(token_total_count) - (level_count - 4.0) / 3.0 * math.log(4.0)
    return jnp.exp(jnp.where(level_count <= 4.0, quick_log, gentle))


def decay_factors(head_decay_code, token_step_code, forget_token_code, token_total_count):
    every_rate = head_rates(head_decay_code, token_total_count)
    token_step_sizes = jnp.sqrt(2.0 * every_rate)[:, None] * jnp.exp(
        math.log(2.0) * (0.5 * token_step_code.astype(jnp.float32) - 0.75)
    )
    logarithm_decay = (
        -jnp.sqrt(0.5 * every_rate)[:, None] * token_step_sizes
        - 0.2 * forget_token_code.astype(jnp.float32)[None, :]
    )
    return (token_step_sizes, logarithm_decay)


def column_of(table, index):
    lanes = lax.broadcasted_iota(jnp.int32, table.shape, 1)
    return jnp.sum(jnp.where(lanes == index, table, 0.0), axis=1, keepdims=True)


def end_state_kernel(x_ref, write_ref, weight_ref, state_ref):
    weight = column_of(weight_ref[...], pl.program_id(0))
    weighted = (write_ref[...].astype(jnp.float32) * weight).astype(jnp.bfloat16)
    state_ref[0] = lax.dot_general(
        weighted, x_ref[...], (((0,), (0,)), ((), ())), preferred_element_type=jnp.float32
    )


def mixer_kernel(
    x_ref, gate_ref, write_ref, read_ref, cum_row_ref, size_row_ref, cum_table_ref, gain_ref,
    incoming_ref, gated_ref, square_ref, cross_ref,
):
    head = pl.program_id(0)
    rows = x_ref.shape[0]
    half = rows // 2

    @pl.when(head == 0)
    def _():
        cross_ref[...] = lax.dot_general(
            read_ref[...], write_ref[...], (((1,), (1,)), ((), ())),
            preferred_element_type=jnp.float32,
        )
        square_ref[...] = jnp.zeros_like(square_ref)

    cum_column = column_of(cum_table_ref[...], head)
    direct = column_of(gain_ref[...], head)
    incoming = incoming_ref[0]
    for part in range(2):
        here = slice(part * half, (part + 1) * half)
        upto = (part + 1) * half
        x_here = x_ref[here, :]
        row_ids = part * half + lax.broadcasted_iota(jnp.int32, (half, upto), 0)
        column_ids = lax.broadcasted_iota(jnp.int32, (half, upto), 1)
        lower = row_ids >= column_ids
        gap = cum_column[here] - cum_row_ref[0, :, :upto]
        mixing = jnp.where(
            lower,
            jnp.exp(jnp.where(lower, gap, 0.0))
            * cross_ref[here, :upto]
            * size_row_ref[0, :, :upto],
            0.0,
        ).astype(jnp.bfloat16)
        mixed = jnp.dot(mixing, x_ref[:upto, :], preferred_element_type=jnp.float32)
        mixed += jnp.exp(cum_column[here]) * jnp.dot(
            read_ref[here, :], incoming, preferred_element_type=jnp.float32
        )
        mixed += direct * x_here.astype(jnp.float32)
        gate = gate_ref[here, :].astype(jnp.float32)
        gated = mixed * (gate / (1.0 + jnp.exp(-gate)))
        gated_ref[here, :] = gated
        square_ref[here, :] += jnp.sum(gated * gated, axis=1, keepdims=True)


def attention_kernel(group, q_ref, *refs):
    key_refs, value_refs, out_ref = refs[: group + 1], refs[group + 1 : -1], refs[-1]
    rows = q_ref.shape[0]
    half = rows // 2
    position = lax.axis_index("ctx")
    mine = position % group
    has_before = position >= group
    scale = HD ** (-0.5)
    for part in range(2):
        query = q_ref[part * half : (part + 1) * half, :]
        spans = [slice(0, (part + 1) * half)]
        spans += [slice(0, rows)] * (group - 1)
        spans += [slice(part * half, rows)]
        all_scores = []
        for which, span in enumerate(spans):
            scores = lax.dot_general(
                query, key_refs[which][span, :], (((1,), (1,)), ((), ())),
                preferred_element_type=jnp.float32,
            )
            if which == 0 or which == group:
                query_ids = part * half + lax.broadcasted_iota(jnp.int32, scores.shape, 0)
                key_ids = span.start + lax.broadcasted_iota(jnp.int32, scores.shape, 1)
                if which == 0:
                    scores = jnp.where(key_ids <= query_ids, scores, -jnp.inf)
                else:
                    kept = jnp.logical_and(key_ids > query_ids, has_before)
                    scores = jnp.where(kept, scores, -jnp.inf)
            else:
                kept = jnp.logical_or(jnp.bitwise_xor(mine, which) < mine, has_before)
                scores = jnp.where(kept, scores, -jnp.inf)
            all_scores.append(scores)
        maximum = functools.reduce(
            jnp.maximum, [jnp.max(scores, axis=1, keepdims=True) for scores in all_scores]
        )
        total = jnp.zeros_like(maximum)
        attended = jnp.zeros((half, HD), jnp.float32)
        for which, span in enumerate(spans):
            weights = jnp.exp((all_scores[which] - maximum) * scale)
            total += jnp.sum(weights, axis=1, keepdims=True)
            attended += jnp.dot(
                weights.astype(jnp.bfloat16), value_refs[which][span, :],
                preferred_element_type=jnp.float32,
            )
        out_ref[part * half : (part + 1) * half, :] = (attended / total).astype(jnp.bfloat16)


def attend(query, pairs, first_head, heads, group):
    rows = query.shape[0]
    block = (rows, HD)
    return pl.pallas_call(
        functools.partial(attention_kernel, group),
        grid=(heads,),
        in_specs=[pl.BlockSpec(block, lambda h: (0, first_head + h))]
        + [pl.BlockSpec(block, lambda h: (0, h))] * (group + 1)
        + [pl.BlockSpec(block, lambda h: (0, heads + h))] * (group + 1),
        out_specs=pl.BlockSpec(block, lambda h: (0, h)),
        out_shape=jax.ShapeDtypeStruct((rows, heads * HD), jnp.bfloat16),
        compiler_params=pltpu.CompilerParams(vmem_limit_bytes=VMEM_LIMIT),
        cost_estimate=pl.CostEstimate(
            flops=4 * heads * rows * rows * (group + 1) * HD,
            bytes_accessed=2 * heads * rows * HD * (2 * group + 4),
            transcendentals=heads * rows * rows * (group + 1),
        ),
    )(query, *pairs, *pairs)


def per_device(
    space_head_input,
    mixer_gate_input,
    state_write_matrix,
    readout_matrix,
    head_decay_code,
    token_step_code,
    forget_token_code,
    head_direct_gain,
    output_norm_gain,
    attention_query,
    attention_key,
    attention_value,
):
    rows = space_head_input.shape[0]
    local_heads = head_decay_code.shape[0]
    state_size = state_write_matrix.shape[1]
    count = lax.axis_size("ctx")
    position = lax.axis_index("ctx")
    group = WINDOW // rows
    mine = position % group
    shift = lambda value, steps: lax.ppermute(
        value, "ctx", [(source, source + steps) for source in range(count - steps)]
    )
    swap = lambda value, bits: lax.ppermute(
        value, "ctx", [(source, source ^ bits) for source in range(count)]
    )

    heads = attention_query.shape[1] // HD
    parts = HEAD_GROUPS if heads % HEAD_GROUPS == 0 else 1
    part_heads = heads // parts
    gathered = []
    for part in range(parts):
        columns = slice(part * part_heads * HD, (part + 1) * part_heads * HD)
        own = jnp.concatenate([attention_key[:, columns], attention_value[:, columns]], axis=1)
        before = shift(own, group)
        sent = {}
        bit = 1
        while bit < group:
            sent[bit] = jnp.where(jnp.bitwise_and(mine, bit) == 0, own, before)
            bit *= 2
        pairs = [own]
        for bits in range(1, group):
            top = 1 << (bits.bit_length() - 1)
            pairs.append(swap(sent[top], bits))
        gathered.append(pairs + [before])

    sizes, log_decay = decay_factors(
        head_decay_code, token_step_code, forget_token_code, rows * count
    )
    upper = (jnp.arange(rows)[:, None] <= jnp.arange(rows)[None, :]).astype(jnp.float32)
    cumulative = jnp.dot(log_decay, upper, precision=lax.Precision.HIGHEST)
    last = cumulative[:, -1]
    logs = lax.all_gather(last, "ctx")
    weights = jnp.exp(last[:, None] - cumulative) * sizes

    state = pl.pallas_call(
        end_state_kernel,
        grid=(local_heads,),
        in_specs=[
            pl.BlockSpec((rows, P_SIZE), lambda h: (0, h)),
            pl.BlockSpec((rows, state_size), lambda h: (0, 0)),
            pl.BlockSpec((rows, local_heads), lambda h: (0, 0)),
        ],
        out_specs=pl.BlockSpec((1, state_size, P_SIZE), lambda h: (h, 0, 0)),
        out_shape=jax.ShapeDtypeStruct((local_heads, state_size, P_SIZE), jnp.float32),
        cost_estimate=pl.CostEstimate(
            flops=2 * local_heads * rows * state_size * P_SIZE,
            bytes_accessed=2 * local_heads * rows * P_SIZE,
            transcendentals=0,
        ),
    )(space_head_input, state_write_matrix, weights.T)

    device_ids = jnp.arange(count)

    def decay_over(first, stop):
        inside = (device_ids >= first) & (device_ids < stop)
        return jnp.exp(jnp.sum(jnp.where(inside[:, None], logs, 0.0), axis=0))[:, None, None]

    prefix = jnp.zeros_like(state)
    total = state
    bit = 1
    while bit < group:
        other = swap(total.astype(jnp.bfloat16), bit).astype(jnp.float32)
        start = position - position % bit
        later = jnp.bitwise_and(position, bit) != 0
        partner = jnp.bitwise_xor(start, bit)
        prefix = jnp.where(later, prefix + decay_over(start, position) * other, prefix)
        total = jnp.where(
            later,
            total + decay_over(start, start + bit) * other,
            other + decay_over(partner, partner + bit) * total,
        )
        bit *= 2
    group_start = position - mine
    earlier = shift(total.astype(jnp.bfloat16), group).astype(jnp.float32)
    span = 1
    while span * group < count - group:
        more = shift(earlier.astype(jnp.bfloat16), span * group).astype(jnp.float32)
        earlier = earlier + decay_over(group_start - span * group, group_start) * more
        span *= 2
    incoming = (prefix + decay_over(group_start, position) * earlier).astype(jnp.bfloat16)

    gated, squares = pl.pallas_call(
        mixer_kernel,
        grid=(local_heads,),
        in_specs=[
            pl.BlockSpec((rows, P_SIZE), lambda h: (0, h)),
            pl.BlockSpec((rows, P_SIZE), lambda h: (0, h)),
            pl.BlockSpec((rows, state_size), lambda h: (0, 0)),
            pl.BlockSpec((rows, state_size), lambda h: (0, 0)),
            pl.BlockSpec((1, 1, rows), lambda h: (h, 0, 0)),
            pl.BlockSpec((1, 1, rows), lambda h: (h, 0, 0)),
            pl.BlockSpec((rows, local_heads), lambda h: (0, 0)),
            pl.BlockSpec((1, local_heads), lambda h: (0, 0)),
            pl.BlockSpec((1, state_size, P_SIZE), lambda h: (h, 0, 0)),
        ],
        out_specs=[
            pl.BlockSpec((rows, P_SIZE), lambda h: (0, h)),
            pl.BlockSpec((rows, 1), lambda h: (0, 0)),
        ],
        out_shape=[
            jax.ShapeDtypeStruct((rows, local_heads * P_SIZE), jnp.float32),
            jax.ShapeDtypeStruct((rows, 1), jnp.float32),
        ],
        scratch_shapes=[pltpu.VMEM((rows, rows), jnp.float32)],
        compiler_params=pltpu.CompilerParams(vmem_limit_bytes=VMEM_LIMIT),
        cost_estimate=pl.CostEstimate(
            flops=2 * local_heads * rows * (rows + state_size) * P_SIZE,
            bytes_accessed=8 * local_heads * rows * P_SIZE,
            transcendentals=local_heads * rows * (rows + P_SIZE),
        ),
    )(
        space_head_input,
        mixer_gate_input,
        state_write_matrix,
        readout_matrix,
        cumulative[:, None, :],
        sizes[:, None, :],
        cumulative.T,
        head_direct_gain[None, :],
        incoming,
    )
    squares = lax.psum(squares[:, 0], "head")
    mixer_out = (
        gated * lax.rsqrt(squares[:, None] / (SSM_HEADS * P_SIZE) + 1e-05) * output_norm_gain
    ).astype(jnp.bfloat16)

    outs = [
        attend(attention_query, gathered[part], part * part_heads, part_heads, group)
        for part in range(parts)
    ]
    window_out = outs[0] if parts == 1 else jnp.concatenate(outs, axis=1)
    return (mixer_out, window_out)


def solution(mesh):
    return jax.shard_map(
        per_device,
        mesh=mesh,
        in_specs=(
            P("ctx", "head"),
            P("ctx", "head"),
            P("ctx", None),
            P("ctx", None),
            P("head"),
            P("head", "ctx"),
            P("ctx"),
            P("head"),
            P("head"),
            P("ctx", "head"),
            P("ctx", "head"),
            P("ctx", "head"),
        ),
        out_specs=(P("ctx", "head"), P("ctx", "head")),
        check_vma=False,
    )
```

time: 724 us -> 300 us (0.41)
  blocking collectives: 341 us -> 42.8 us
  matrix products: 88.5 us -> 0.34 us
  Pallas kernels: 0 us -> 51.6 us
  local copies, waits for them, and re-layouts: 55.2 us -> 10.7 us
  other arithmetic: 62.1 us -> 26.6 us
  waiting for transfers between devices: 116 us -> 145 us
  starting transfers between devices: 37.3 us -> 17.9 us
  between operations: 15.9 us -> 1.77 us
    unnamed x1, blocking collectives: 334 us -> 38 us
    dot_general x28 -> x1, matrix products: 88.5 us -> 0.34 us  [per_device(): cumulative = jnp.dot(log_decay, upper, precision=lax.Precision.HIGHEST)]
    pallas_call x0 -> x4, Pallas kernels: none -> 51.6 us  [the longest x2 30.1 us: attend(): pl.pallas_call(functools.partial(attention_kernel, group), grid=(heads,),...]
    ppermute x8 -> x13, waiting for transfers between devices: 116 us -> 145 us  [the longest x8 104 us: per_device(): lax.ppermute(value, 'ctx', [(source, source ^ bits) for source in range(c...]
    unnamed x77 -> x51, local copies, waits for them, and re-layouts: 34.2 us -> 6.05 us
    select_n x15 -> x2, other arithmetic: 30.5 us -> 7.32 us  [per_device(): sent[bit] = jnp.where(jnp.bitwise_and(mine, bit) == 0, own, before)]
    ppermute x8 -> x13, starting transfers between devices: 37.2 us -> 17.9 us  [the longest x5 11.1 us: per_device(): lax.ppermute(value, 'ctx', [(source, source + steps) for source in range(...]
    reduce_sum x13 -> x1, other arithmetic: 18.9 us -> 0.11 us  [decay_over(): jnp.sum(jnp.where(inside[:, None], logs, 0.0), axis=0)]
  transfers between devices with their start and end apart: 9 -> 13, of which waited for: 3 -> 5; matrix products, arithmetic and copies ran while one was open for 15% -> 7% of each run, Pallas kernels for 0% -> 13%
where the time goes in v1:
time: 300 us; the launch traced here: 297 us
  waiting for transfers between devices  145 us (48%)
  Pallas kernels  51.6 us (17%)
  blocking collectives  42.8 us (14%)
  other arithmetic  26.6 us (9%)
  starting transfers between devices  17.9 us (6%)
  local copies, waits for them, and re-layouts  10.7 us (4%)
    ppermute x8, waiting for transfers between devices, per_device(): lax.ppermute(value, 'ctx', [(source, source ^ bits) for source in range(c...  104 us
    ppermute x5, waiting for transfers between devices, per_device(): lax.ppermute(value, 'ctx', [(source, source + steps) for source in range(...  41.4 us
    unnamed x1, blocking collectives  38 us
    pallas_call x2, Pallas kernels, attend(): pl.pallas_call(functools.partial(attention_kernel, group), grid=(heads,),...  30.1 us
    pallas_call x1, Pallas kernels, per_device(): pl.pallas_call(mixer_kernel, grid=(local_heads,), in_specs=[pl.BlockSpec(...  11.9 us
    ppermute x5, starting transfers between devices, per_device(): lax.ppermute(value, 'ctx', [(source, source + steps) for source in range(...  11.1 us
    pallas_call x1, Pallas kernels, per_device(): pl.pallas_call(end_state_kernel, grid=(local_heads,), in_specs=[pl.BlockS...  9.63 us
    select_n x2, other arithmetic, per_device(): sent[bit] = jnp.where(jnp.bitwise_and(mine, bit) == 0, own, before)  7.32 us
  transfers between devices with their start and end apart: 13, of which 5 were waited for; matrix products, arithmetic and copies ran while one was open for 7% of the time, Pallas kernels for 13%

profile of v1, /device:TPU:9, one launch (start us, length us, event | category | flops | bytes accessed | tf_op | source)
XLA Modules:
  0.0 296.6 jit_solution(11058051523631854104)
XLA Ops:
  0.6 3.3 %fusion.17 = (bf16[512,768]{1,0:T(8,128)(2,1)S(1)}, bf16[512,768]{1,0:T(8,128)(2,1)}, bf16[512,768]{1,0:T(8,128)(2,1)}, bf16[512,768]{1,0:T(8,128)(2,1)S(1)}) fusion(bf16[512,1536]{1,0:T(8,128)(2,1)} %param.22, bf16[512,1536]{1,0:T(8,128)(2,1)} %param.23), kind=kLoop, calls=%fused_computation.60 | loop fusion | bytes 6291456 | tf_op jit(solution)/shard_map/slice | solution.py:196
  5.1 3.2 %collective-permute-start.5 = (bf16[512,1536]{1,0:T(8,128)(2,1)S(1)}, bf16[512,1536]{1,0:T(8,128)(2,1)}, u32[]{:S(2)}, u32[]{:S(2)}) collective-permute-start(bf16[512,1536]{1,0:T(8,128)(2,1)S(1)} %pad_maximum_fusion.refs_0_.refs_5_), channel_id=1, source_target_pairs={{0,8},{2,10},{4,12},{6,14},{8,16},{10,18},{12,20},{14,22},{16,24},... | collective-permute-start | bytes 4718600 | tf_op jit(solution)/shard_map/ppermute | solution.py:183
  9.9 9.6 %shard_map.131 = f32[12,128,256]{2,1,0:T(8,128)} custom-call(bf16[512,3072]{1,0:T(8,128)(2,1)} %x_ref.3, bf16[512,128]{1,0:T(8,128)(2,1)} %write_ref.3, f32[512,12]{1,0:T(8,128)} %copy.19.weight_ref), custom_call_target="tpu_custom_call" | custom-call | flops 402653184 | bytes 3145728 | tf_op jit(solution)/shard_map/pallas_call | solution.py:218
  19.5 2.5 convert_element_type.47
  24.7 38.0 %all-reduce = f32[192]{0:T(256)S(1)} all-reduce(f32[192]{0:T(256)S(1)} %dynamic-update-slice), channel_id=2, replica_groups=mesh['ctx'=16,'head'=2] {'ctx'}, use_global_device_ids=true, to_apply=%add | all-reduce | flops 192 | bytes 1536
  63.1 2.6 fusion.15
  65.8 1.9 collective-permute-start.9
  67.8 3.7 %broadcast_select_fusion.1 = (bf16[512,1536]{1,0:T(8,128)(2,1)}, bf16[512,1536]{1,0:T(8,128)(2,1)S(1)}) fusion(bf16[512,1536]{1,0:T(8,128)(2,1)} %collective-permute-done.5.refs_4_.refs_9_, pred[]{:T(512)S(6)} %eq.13, bf16[512,768]{1,0:T(8,128)(2,1)} %copy-done.14, bf16[512,768]{1,0:T(8,128)(2,1)} %copy-done.13, pred[]{:T(512)S(6)} %eq.12), kind=kLoop, calls=%fused_computation.21 | loop fusion | flops 4718592 | bytes 6291458 | tf_op jit(solution)/shard_map/jit(_where)/select_n | solution.py:201
  73.2 3.7 %collective-permute-done.1 = bf16[12,128,256]{2,1,0:T(8,128)(2,1)} collective-permute-done((bf16[12,128,256]{2,1,0:T(8,128)(2,1)}, bf16[12,128,256]{2,1,0:T(8,128)(2,1)}, u32[]{:S(2)}, u32[]{:S(2)}) %collective-permute-start.1) | collective-permute-done | bytes 786464 | tf_op jit(solution)/shard_map/ppermute | solution.py:186
  76.9 2.2 fusion.5
  79.0 2.5 collective-permute-start.2
  81.6 35.5 %collective-permute-done.2 = bf16[12,128,256]{2,1,0:T(8,128)(2,1)S(1)} collective-permute-done((bf16[12,128,256]{2,1,0:T(8,128)(2,1)S(1)}, bf16[12,128,256]{2,1,0:T(8,128)(2,1)S(1)}, u32[]{:S(2)}, u32[]{:S(2)}) %collective-permute-start.2) | collective-permute-done | bytes 786464 | tf_op jit(solution)/shard_map/ppermute | solution.py:183
  117.0 1.9 collective-permute-start.3
  120.2 3.6 %broadcast_select_fusion = (bf16[512,1536]{1,0:T(8,128)(2,1)}, bf16[512,1536]{1,0:T(8,128)(2,1)}) fusion(bf16[512,1536]{1,0:T(8,128)(2,1)} %collective-permute-done.9.refs_4_.refs_9_, pred[]{:T(512)S(6)} %eq.13, bf16[512,768]{1,0:T(8,128)(2,1)S(1)} %copy-done.12, bf16[512,768]{1,0:T(8,128)(2,1)S(1)} %copy-done.10, pred[]{:T(512)S(6)} %eq.12), kind=kLoop, calls=%fused_computation.20 | loop fusion | flops 4718592 | bytes 6291458 | tf_op jit(solution)/shard_map/jit(_where)/select_n | solution.py:201
  127.7 5.9 %collective-permute-done.3 = bf16[12,128,256]{2,1,0:T(8,128)(2,1)S(1)} collective-permute-done((bf16[12,128,256]{2,1,0:T(8,128)(2,1)S(1)}, bf16[12,128,256]{2,1,0:T(8,128)(2,1)S(1)}, u32[]{:S(2)}, u32[]{:S(2)}) %collective-permute-start.3) | collective-permute-done | bytes 786464 | tf_op jit(solution)/shard_map/ppermute | solution.py:183
  134.8 1.8 fusion.8
  136.6 60.8 %collective-permute-done.7.refs_2_.refs_7_ = bf16[512,1536]{1,0:T(8,128)(2,1)} collective-permute-done((bf16[512,1536]{1,0:T(8,128)(2,1)}, bf16[512,1536]{1,0:T(8,128)(2,1)}, u32[]{:S(2)}, u32[]{:S(2)}) %collective-permute-start.7) | collective-permute-done | bytes 1572896 | tf_op jit(solution)/shard_map/ppermute | solution.py:186
  200.3 15.1 %shard_map.133 = bf16[512,768]{1,0:T(8,128)(2,1)S(1)} custom-call(bf16[512,1536]{1,0:T(8,128)(2,1)S(1)} %copy-done, bf16[512,1536]{1,0:T(8,128)(2,1)S(1)} %pad_maximum_fusion.refs_0_.refs_5_, bf16[512,1536]{1,0:T(8,128)(2,1)S(1)} %copy-done.2, bf16[512,1536]{1,0:T(8,128)(2,1)} %collective-permute-done.7.refs_2_.refs_7_, ...), custom_call_target="tpu_custom_call" | custom-call | flops 4026531840 | bytes 9437184 | tf_op jit(solution)/shard_map/pallas_call | solution.py:145
  215.5 39.1 %collective-permute-done.11.refs_2_.refs_7_ = bf16[512,1536]{1,0:T(8,128)(2,1)} collective-permute-done((bf16[512,1536]{1,0:T(8,128)(2,1)}, bf16[512,1536]{1,0:T(8,128)(2,1)}, u32[]{:S(2)}, u32[]{:S(2)}) %collective-permute-start.11) | collective-permute-done | bytes 1572896 | tf_op jit(solution)/shard_map/ppermute | solution.py:186
  254.6 15.0 %shard_map.134 = bf16[512,768]{1,0:T(8,128)(2,1)S(1)} custom-call(bf16[512,1536]{1,0:T(8,128)(2,1)S(1)} %copy-done, bf16[512,1536]{1,0:T(8,128)(2,1)S(1)} %pad_maximum_fusion.1.refs_0_.refs_5_, bf16[512,1536]{1,0:T(8,128)(2,1)} %collective-permute-done.10.refs_1_.refs_6_, bf16[512,1536]{1,0:T(8,128)(2,1)} %collective-permute-done.11.refs_2_.refs_7_, ...), custom_call_target="tpu_custom_call" | custom-call | flops 4026531840 | bytes 9437184 | tf_op jit(solution)/shard_map/pallas_call | solution.py:145
  271.6 2.8 fusion.7.incoming_ref
  274.4 11.9 %shard_map.132 = (f32[512,3072]{1,0:T(8,128)}, f32[512,1]{1,0:T(8,128)S(1)}) custom-call(bf16[512,3072]{1,0:T(8,128)(2,1)S(1)} %copy-done.3, bf16[512,3072]{1,0:T(8,128)(2,1)} %gate_ref.1, bf16[512,128]{1,0:T(8,128)(2,1)S(1)} %copy-done.4, bf16[512,128]{1,0:T(8,128)(2,1)S(1)} %copy-done.5, f32[12,1,512]{2,1,0:T(1,128)S(1)} %broadcast_in_dim.97.cum_row_ref, ...), custom_call_target="tpu_custom_call" | custom-call | flops 2013265920 | bytes 12582912 | tf_op jit(solution)/shard_map/pallas_call | solution.py:265
  286.4 4.8 %psum.7 = f32[512]{0:T(512)S(1)} all-reduce(f32[512]{0:T(512)S(1)} %reduce.1), channel_id=1, replica_groups=mesh['ctx'=16,'head'=2] {'head'}, use_global_device_ids=true, to_apply=%region_9.10 | all-reduce | flops 512 | bytes 4096 | tf_op jit(solution)/shard_map/psum | solution.py:305
  291.2 5.5 %multiply_convert_fusion = bf16[512,3072]{1,0:T(8,128)(2,1)} fusion(f32[512,3072]{1,0:T(8,128)} %get-tuple-element.4, f32[3072]{0:T(1024)S(1)} %copy-done.20, f32[512]{0:T(512)S(1)} %add_rsqrt_fusion), kind=kLoop, calls=%fused_computation | loop fusion | flops 4718592 | bytes 9451520 | tf_op jit(solution)/shard_map/convert_element_type | solution.py:308
  (100 shorter events, 18.1 us)
Async XLA Ops:
  3.9 4.4 %copy-start.22 = (s32[12]{0:T(128)S(1)}, s32[12]{0:T(128)}, u32[]{:S(2)}) copy-start(s32[12]{0:T(128)} %param.16) | copy-start | bytes 148
  3.9 4.4 %copy-start.21 = (s32[512]{0:T(512)S(1)}, s32[512]{0:T(512)}, u32[]{:S(2)}) copy-start(s32[512]{0:T(512)} %param.18) | copy-start | bytes 6148
  3.9 4.4 %copy-start.19 = (s32[12,512]{1,0:T(8,128)S(1)}, s32[12,512]{1,0:T(8,128)}, u32[]{:S(2)}) copy-start(s32[12,512]{1,0:T(8,128)} %param.17) | copy-start | bytes 73732
  5.1 62.7 %collective-permute-start.5 = (bf16[512,1536]{1,0:T(8,128)(2,1)S(1)}, bf16[512,1536]{1,0:T(8,128)(2,1)}, u32[]{:S(2)}, u32[]{:S(2)}) collective-permute-start(bf16[512,1536]{1,0:T(8,128)(2,1)S(1)} %pad_maximum_fusion.refs_0_.refs_5_), channel_id=1, source_target_pairs={{0,8},{2,10},{4,12},{6,14},{8,16},{10,18},{12,20},{14,22},{16,24},... | collective-permute-start | bytes 4718600 | tf_op jit(solution)/shard_map/ppermute | solution.py:183
  19.5 3.7 %copy-start.23 = (u32[32]{0:T(128)S(1)}, u32[32]{0:T(128)}, u32[]{:S(2)}) copy-start(u32[32]{0:T(128)} %constant.83) | copy-start | bytes 388
  19.5 43.5 %copy-start.7 = (f32[12,128,256]{2,1,0:T(8,128)S(1)}, f32[12,128,256]{2,1,0:T(8,128)}, u32[]{:S(2)}) copy-start(f32[12,128,256]{2,1,0:T(8,128)} %shard_map.131) | copy-start | bytes 4718596
  22.0 41.0 %collective-permute-start = (bf16[12,128,256]{2,1,0:T(8,128)(2,1)}, bf16[12,128,256]{2,1,0:T(8,128)(2,1)}, u32[]{:S(2)}, u32[]{:S(2)}) collective-permute-start(bf16[12,128,256]{2,1,0:T(8,128)(2,1)} %convert_element_type.47), channel_id=1, source_target_pairs={{0,2},{2,0},{4,6},{6,4},{8,10},{10,8},{12,14},{14,12},{16,18},{18,... | collective-permute-start | bytes 2359304 | tf_op jit(solution)/shard_map/ppermute | solution.py:186
  65.7 11.2 %collective-permute-start.1 = (bf16[12,128,256]{2,1,0:T(8,128)(2,1)}, bf16[12,128,256]{2,1,0:T(8,128)(2,1)}, u32[]{:S(2)}, u32[]{:S(2)}) collective-permute-start(bf16[12,128,256]{2,1,0:T(8,128)(2,1)} %fusion.15), channel_id=1, source_target_pairs={{0,4},{2,6},{4,0},{6,2},{8,12},{10,14},{12,8},{14,10},{16,20},{18,... | collective-permute-start | bytes 2359304 | tf_op jit(solution)/shard_map/ppermute | solution.py:186
  65.8 54.4 %collective-permute-start.9 = (bf16[512,1536]{1,0:T(8,128)(2,1)S(1)}, bf16[512,1536]{1,0:T(8,128)(2,1)}, u32[]{:S(2)}, u32[]{:S(2)}) collective-permute-start(bf16[512,1536]{1,0:T(8,128)(2,1)S(1)} %pad_maximum_fusion.1.refs_0_.refs_5_), channel_id=1, source_target_pairs={{0,8},{2,10},{4,12},{6,14},{8,16},{10,18},{12,20},{14,22},{16,24},... | collective-permute-start | bytes 4718600 | tf_op jit(solution)/shard_map/ppermute | solution.py:183
  67.8 9.1 %copy-start.8 = (f32[12,128,256]{2,1,0:T(8,128)S(1)}, f32[12,128,256]{2,1,0:T(8,128)}, u32[]{:S(2)}) copy-start(f32[12,128,256]{2,1,0:T(8,128)} %shard_map.131) | copy-start | bytes 4718596
  71.5 48.7 %copy-start.10 = (bf16[512,768]{1,0:T(8,128)(2,1)S(1)}, bf16[512,768]{1,0:T(8,128)(2,1)}, u32[]{:S(2)}) copy-start(bf16[512,768]{1,0:T(8,128)(2,1)} %get-tuple-element.22) | copy-start | bytes 2359300
  71.5 48.7 %copy-start.12 = (bf16[512,768]{1,0:T(8,128)(2,1)S(1)}, bf16[512,768]{1,0:T(8,128)(2,1)}, u32[]{:S(2)}) copy-start(bf16[512,768]{1,0:T(8,128)(2,1)} %get-tuple-element.33) | copy-start | bytes 2359300
  71.5 53.8 %collective-permute-start.6 = (bf16[512,1536]{1,0:T(8,128)(2,1)S(1)}, bf16[512,1536]{1,0:T(8,128)(2,1)S(1)}, u32[]{:S(2)}, u32[]{:S(2)}) collective-permute-start(bf16[512,1536]{1,0:T(8,128)(2,1)S(1)} %get-tuple-element.18), channel_id=1, source_target_pairs={{0,2},{2,0},{4,6},{6,4},{8,10},{10,8},{12,14},{14,12},{16,18},{18,... | collective-permute-start | bytes 4718600 | tf_op jit(solution)/shard_map/ppermute | solution.py:186
  79.0 38.0 %collective-permute-start.2 = (bf16[12,128,256]{2,1,0:T(8,128)(2,1)S(1)}, bf16[12,128,256]{2,1,0:T(8,128)(2,1)S(1)}, u32[]{:S(2)}, u32[]{:S(2)}) collective-permute-start(bf16[12,128,256]{2,1,0:T(8,128)(2,1)S(1)} %fusion.5), channel_id=1, source_target_pairs={{0,8},{2,10},{4,12},{6,14},{8,16},{10,18},{12,20},{14,22},{16,24},... | collective-permute-start | bytes 2359304 | tf_op jit(solution)/shard_map/ppermute | solution.py:183
  117.0 6.8 %copy-start.15 = (bf16[12,128,256]{2,1,0:T(8,128)(2,1)}, bf16[12,128,256]{2,1,0:T(8,128)(2,1)S(1)}, u32[]{:S(2)}) copy-start(bf16[12,128,256]{2,1,0:T(8,128)(2,1)S(1)} %collective-permute-done.2) | copy-start | bytes 2359300
  117.0 16.5 %collective-permute-start.3 = (bf16[12,128,256]{2,1,0:T(8,128)(2,1)S(1)}, bf16[12,128,256]{2,1,0:T(8,128)(2,1)S(1)}, u32[]{:S(2)}, u32[]{:S(2)}) collective-permute-start(bf16[12,128,256]{2,1,0:T(8,128)(2,1)S(1)} %collective-permute-done.2), channel_id=1, source_target_pairs={{0,8},{2,10},{4,12},{6,14},{8,16},{10,18},{12,20},{14,22},{16,24},... | collective-permute-start | bytes 2359304 | tf_op jit(solution)/shard_map/ppermute | solution.py:183
  119.0 78.4 %collective-permute-start.7 = (bf16[512,1536]{1,0:T(8,128)(2,1)}, bf16[512,1536]{1,0:T(8,128)(2,1)}, u32[]{:S(2)}, u32[]{:S(2)}) collective-permute-start(bf16[512,1536]{1,0:T(8,128)(2,1)} %get-tuple-element.17), channel_id=1, source_target_pairs={{0,4},{2,6},{4,0},{6,2},{8,12},{10,14},{12,8},{14,10},{16,20},{18,... | collective-permute-start | bytes 4718600 | tf_op jit(solution)/shard_map/ppermute | solution.py:186
  120.2 78.7 %collective-permute-start.8 = (bf16[512,1536]{1,0:T(8,128)(2,1)}, bf16[512,1536]{1,0:T(8,128)(2,1)}, u32[]{:S(2)}, u32[]{:S(2)}) collective-permute-start(bf16[512,1536]{1,0:T(8,128)(2,1)} %get-tuple-element.17), channel_id=1, source_target_pairs={{0,6},{2,4},{4,2},{6,0},{8,14},{10,12},{12,10},{14,8},{16,22},{18,... | collective-permute-start | bytes 4718600 | tf_op jit(solution)/shard_map/ppermute | solution.py:186
  123.9 91.6 %collective-permute-start.10 = (bf16[512,1536]{1,0:T(8,128)(2,1)}, bf16[512,1536]{1,0:T(8,128)(2,1)}, u32[]{:S(2)}, u32[]{:S(2)}) collective-permute-start(bf16[512,1536]{1,0:T(8,128)(2,1)} %get-tuple-element.20), channel_id=1, source_target_pairs={{0,2},{2,0},{4,6},{6,4},{8,10},{10,8},{12,14},{14,12},{16,18},{18,... | collective-permute-start | bytes 4718600 | tf_op jit(solution)/shard_map/ppermute | solution.py:186
  126.5 128.1 %collective-permute-start.11 = (bf16[512,1536]{1,0:T(8,128)(2,1)}, bf16[512,1536]{1,0:T(8,128)(2,1)}, u32[]{:S(2)}, u32[]{:S(2)}) collective-permute-start(bf16[512,1536]{1,0:T(8,128)(2,1)} %get-tuple-element.19), channel_id=1, source_target_pairs={{0,4},{2,6},{4,0},{6,2},{8,12},{10,14},{12,8},{14,10},{16,20},{18,... | collective-permute-start | bytes 4718600 | tf_op jit(solution)/shard_map/ppermute | solution.py:186
  134.5 120.1 %collective-permute-start.12 = (bf16[512,1536]{1,0:T(8,128)(2,1)}, bf16[512,1536]{1,0:T(8,128)(2,1)}, u32[]{:S(2)}, u32[]{:S(2)}) collective-permute-start(bf16[512,1536]{1,0:T(8,128)(2,1)} %get-tuple-element.19), channel_id=1, source_target_pairs={{0,6},{2,4},{4,2},{6,0},{8,14},{10,12},{12,10},{14,8},{16,22},{18,... | collective-permute-start | bytes 4718600 | tf_op jit(solution)/shard_map/ppermute | solution.py:186
  134.6 64.3 %copy-start = (bf16[512,1536]{1,0:T(8,128)(2,1)S(1)}, bf16[512,1536]{1,0:T(8,128)(2,1)}, u32[]{:S(2)}) copy-start(bf16[512,1536]{1,0:T(8,128)(2,1)} %q_ref.3) | copy-start | bytes 4718596
  197.4 73.5 %collective-permute-start.4 = (bf16[12,128,256]{2,1,0:T(8,128)(2,1)S(1)}, bf16[12,128,256]{2,1,0:T(8,128)(2,1)S(1)}, u32[]{:S(2)}, u32[]{:S(2)}) collective-permute-start(bf16[12,128,256]{2,1,0:T(8,128)(2,1)S(1)} %fusion.8), channel_id=1, source_target_pairs={{0,16},{2,18},{4,20},{6,22},{8,24},{10,26},{12,28},{14,30},{1,17},... | collective-permute-start | bytes 2359304 | tf_op jit(solution)/shard_map/ppermute | solution.py:183
  274.4 16.8 %copy-start.20 = (f32[3072]{0:T(1024)S(1)}, f32[3072]{0:T(1024)}, u32[]{:S(2)}) copy-start(f32[3072]{0:T(1024)} %param.20) | copy-start | bytes 36868
  (13 other events, 27.9 us)

commit v2 on v1

--- a/solution.py
+++ b/solution.py
@@ -13,6 +13,7 @@
 P_SIZE = 256
 WINDOW = 2048
 HEAD_GROUPS = 2
+LOG_ROWS = 16
 VMEM_LIMIT = 48 * 1024 * 1024
 
 
@@ -187,34 +188,24 @@
         value, "ctx", [(source, source ^ bits) for source in range(count)]
     )
 
+    sizes, log_decay = decay_factors(
+        head_decay_code, token_step_code, forget_token_code, rows * count
+    )
+    upper = (jnp.arange(rows)[:, None] <= jnp.arange(rows)[None, :]).astype(jnp.float32)
+    cumulative = jnp.dot(log_decay, upper, precision=lax.Precision.HIGHEST)
+    last = cumulative[:, -1]
+    weights = jnp.exp(last[:, None] - cumulative) * sizes
+
     heads = attention_query.shape[1] // HD
     parts = HEAD_GROUPS if heads % HEAD_GROUPS == 0 else 1
     part_heads = heads // parts
-    gathered = []
+    owns = []
     for part in range(parts):
         columns = slice(part * part_heads * HD, (part + 1) * part_heads * HD)
-        own = jnp.concatenate([attention_key[:, columns], attention_value[:, columns]], axis=1)
-        before = shift(own, group)
-        sent = {}
-        bit = 1
-        while bit < group:
-            sent[bit] = jnp.where(jnp.bitwise_and(mine, bit) == 0, own, before)
-            bit *= 2
-        pairs = [own]
-        for bits in range(1, group):
-            top = 1 << (bits.bit_length() - 1)
-            pairs.append(swap(sent[top], bits))
-        gathered.append(pairs + [before])
-
-    sizes, log_decay = decay_factors(
-        head_decay_code, token_step_code, forget_token_code, rows * count
-    )
-    upper = (jnp.arange(rows)[:, None] <= jnp.arange(rows)[None, :]).astype(jnp.float32)
-    cumulative = jnp.dot(log_decay, upper, precision=lax.Precision.HIGHEST)
-    last = cumulative[:, -1]
-    logs = lax.all_gather(last, "ctx")
-    weights = jnp.exp(last[:, None] - cumulative) * sizes
-
+        owns.append(
+            jnp.concatenate([attention_key[:, columns], attention_value[:, columns]], axis=1)
+        )
+    owns[0], weights = lax.optimization_barrier((owns[0], weights))
     state = pl.pallas_call(
         end_state_kernel,
         grid=(local_heads,),
@@ -232,35 +223,81 @@
         ),
     )(space_head_input, state_write_matrix, weights.T)
 
-    device_ids = jnp.arange(count)
-
-    def decay_over(first, stop):
-        inside = (device_ids >= first) & (device_ids < stop)
-        return jnp.exp(jnp.sum(jnp.where(inside[:, None], logs, 0.0), axis=0))[:, None, None]
+    def pack(value, log):
+        high = log.astype(jnp.bfloat16)
+        rest = log - high.astype(jnp.float32)
+        middle = rest.astype(jnp.bfloat16)
+        low = (rest - middle.astype(jnp.float32)).astype(jnp.bfloat16)
+        terms = jnp.stack([high, middle, low], axis=1)[:, :, None]
+        extra = jnp.pad(terms, ((0, 0), (0, LOG_ROWS - 3), (0, 0)))
+        extra = jnp.broadcast_to(extra, (local_heads, LOG_ROWS, P_SIZE))
+        return jnp.concatenate([value.astype(jnp.bfloat16), extra], axis=1)
+
+    def unpack(packed):
+        terms = packed[:, state_size : state_size + 3, 0].astype(jnp.float32)
+        log = (terms[:, 0] + terms[:, 1]) + terms[:, 2]
+        return packed[:, :state_size].astype(jnp.float32), log
+
+    def grown(log):
+        return jnp.exp(log)[:, None, None]
+
+    befores = [shift(owns[0], group)]
+    gathered = []
+
+    def exchange(part, before, packed):
+        sent = {}
+        bit = 1
+        while bit < group:
+            sent[bit] = jnp.where(jnp.bitwise_and(mine, bit) == 0, owns[part], before)
+            bit *= 2
+        sent, packed = lax.optimization_barrier((sent, packed))
+        pairs = [owns[part]]
+        for bits in range(1, group):
+            top = 1 << (bits.bit_length() - 1)
+            pairs.append(swap(sent[top], bits))
+        gathered.append(pairs + [before])
+        return packed
 
     prefix = jnp.zeros_like(state)
+    prefix_log = jnp.zeros_like(last)
     total = state
+    total_log = last
+    packed = pack(total, total_log)
     bit = 1
     while bit < group:
-        other = swap(total.astype(jnp.bfloat16), bit).astype(jnp.float32)
-        start = position - position % bit
+        hop = swap(packed, bit)
+        if gathered:
+            hop, gathered[-1] = lax.optimization_barrier((hop, gathered[-1]))
+        other, other_log = unpack(hop)
         later = jnp.bitwise_and(position, bit) != 0
-        partner = jnp.bitwise_xor(start, bit)
-        prefix = jnp.where(later, prefix + decay_over(start, position) * other, prefix)
+        prefix = jnp.where(later, prefix + grown(prefix_log) * other, prefix)
+        prefix_log = jnp.where(later, prefix_log + other_log, prefix_log)
         total = jnp.where(
-            later,
-            total + decay_over(start, start + bit) * other,
-            other + decay_over(partner, partner + bit) * total,
-        )
+            later, total + grown(total_log) * other, other + grown(other_log) * total
+        )
+        total_log = total_log + other_log
+        packed = pack(total, total_log)
+        done = len(gathered)
+        if done < parts:
+            before, packed = lax.optimization_barrier((befores[done], packed))
+            if done + 1 < parts:
+                owns[done + 1], before = lax.optimization_barrier((owns[done + 1], before))
+                befores.append(shift(owns[done + 1], group))
+            packed = exchange(done, before, packed)
         bit *= 2
-    group_start = position - mine
-    earlier = shift(total.astype(jnp.bfloat16), group).astype(jnp.float32)
+    while len(gathered) < parts:
+        done = len(gathered)
+        if done + 1 < parts:
+            befores.append(shift(owns[done + 1], group))
+        packed = exchange(done, befores[done], packed)
+    earlier, earlier_log = unpack(shift(packed, group))
     span = 1
     while span * group < count - group:
-        more = shift(earlier.astype(jnp.bfloat16), span * group).astype(jnp.float32)
-        earlier = earlier + decay_over(group_start - span * group, group_start) * more
+        more, more_log = unpack(shift(pack(earlier, earlier_log), span * group))
+        earlier = earlier + grown(earlier_log) * more
+        earlier_log = earlier_log + more_log
         span *= 2
-    incoming = (prefix + decay_over(group_start, position) * earlier).astype(jnp.bfloat16)
+    incoming = (prefix + grown(prefix_log) * earlier).astype(jnp.bfloat16)
 
     gated, squares = pl.pallas_call(
         mixer_kernel,

time: 300 us -> 297 us (0.990)
  blocking collectives: 42.8 us -> 6.02 us
  waiting for transfers between devices: 145 us -> 169 us
  other arithmetic: 26.6 us -> 34.3 us
  starting transfers between devices: 17.9 us -> 25 us
  local copies, waits for them, and re-layouts: 10.7 us -> 6.51 us
    unnamed x1 -> x0, blocking collectives: 38 us -> none
    ppermute x8, waiting for transfers between devices: 104 us -> 126 us  [per_device(): lax.ppermute(value, 'ctx', [(source, source ^ bits) for source in range(c...]
    ppermute x5, starting transfers between devices: 11.1 us -> 17.2 us  [per_device(): lax.ppermute(value, 'ctx', [(source, source + steps) for source in range(...]
    unnamed x51 -> x14, local copies, waits for them, and re-layouts: 6.05 us -> 0.31 us
    concatenate x0 -> x5, other arithmetic: none -> 3.28 us  [pack(): return jnp.concatenate([value.astype(jnp.bfloat16), extra], axis=1)]
    convert_element_type x5 -> x15, other arithmetic: 11.9 us -> 14.1 us  [the longest x4 8.08 us: pack(): return jnp.concatenate([value.astype(jnp.bfloat16), extra], axis=1)]
  transfers between devices with their start and end apart: 13 -> 13, of which waited for: 5 -> 7; matrix products, arithmetic and copies ran while one was open for 7% -> 4% of each run, Pallas kernels for 13% -> 10%
where the time goes in v2:
time: 297 us; the launch traced here: 294 us
  waiting for transfers between devices  169 us (57%)
  Pallas kernels  51.5 us (17%)
  other arithmetic  34.3 us (12%)
  starting transfers between devices  25 us (8%)
  local copies, waits for them, and re-layouts  6.51 us (2%)
  blocking collectives  6.02 us (2%)
    ppermute x8, waiting for transfers between devices, per_device(): lax.ppermute(value, 'ctx', [(source, source ^ bits) for source in range(c...  126 us
    ppermute x5, waiting for transfers between devices, per_device(): lax.ppermute(value, 'ctx', [(source, source + steps) for source in range(...  43.2 us
    pallas_call x2, Pallas kernels, attend(): pl.pallas_call(functools.partial(attention_kernel, group), grid=(heads,),...  30 us
    ppermute x5, starting transfers between devices, per_device(): lax.ppermute(value, 'ctx', [(source, source + steps) for source in range(...  17.2 us
    pallas_call x1, Pallas kernels, per_device(): pl.pallas_call(mixer_kernel, grid=(local_heads,), in_specs=[pl.BlockSpec(...  11.9 us
    pallas_call x1, Pallas kernels, per_device(): pl.pallas_call(end_state_kernel, grid=(local_heads,), in_specs=[pl.BlockS...  9.63 us
    convert_element_type x4, other arithmetic, pack(): return jnp.concatenate([value.astype(jnp.bfloat16), extra], axis=1)  8.08 us
    ppermute x8, starting transfers between devices, per_device(): lax.ppermute(value, 'ctx', [(source, source ^ bits) for source in range(c...  7.81 us
  transfers between devices with their start and end apart: 13, of which 7 were waited for; matrix products, arithmetic and copies ran while one was open for 4% of the time, Pallas kernels for 10%

profile of v2, /device:TPU:9, one launch (start us, length us, event | category | flops | bytes accessed | tf_op | source)
XLA Modules:
  0.0 294.0 jit_solution(1758928867877678751)
XLA Ops:
  7.4 9.6 %shard_map.131 = f32[12,128,256]{2,1,0:T(8,128)} custom-call(bf16[512,3072]{1,0:T(8,128)(2,1)} %x_ref.3, bf16[512,128]{1,0:T(8,128)(2,1)} %write_ref.3, f32[512,12]{1,0:T(8,128)} %copy.87.weight_ref), custom_call_target="tpu_custom_call" | custom-call | flops 402653184 | bytes 3145728 | tf_op jit(solution)/shard_map/pallas_call | solution.py:209
  20.8 3.2 %collective-permute-start.1 = (bf16[512,1536]{1,0:T(8,128)(2,1)S(1)}, bf16[512,1536]{1,0:T(8,128)(2,1)}, u32[]{:S(2)}, u32[]{:S(2)}) collective-permute-start(bf16[512,1536]{1,0:T(8,128)(2,1)S(1)} %get-tuple-element.39.refs_0_.refs_5_), channel_id=1, source_target_pairs={{0,8},{2,10},{4,12},{6,14},{8,16},{10,18},{12,20},{14,22},{16,24},... | collective-permute-start | bytes 4718600 | tf_op jit(solution)/shard_map/ppermute | solution.py:184
  24.0 16.4 %collective-permute-done = bf16[12,144,256]{2,1,0:T(8,128)(2,1)} collective-permute-done((bf16[12,144,256]{2,1,0:T(8,128)(2,1)}, bf16[12,144,256]{2,1,0:T(8,128)(2,1)}, u32[]{:S(2)}, u32[]{:S(2)}) %collective-permute-start) | collective-permute-done | bytes 884768 | tf_op jit(solution)/shard_map/ppermute | solution.py:187
  41.5 2.1 fusion.22
  44.6 13.1 %collective-permute-done.1.refs_4_.refs_9_ = bf16[512,1536]{1,0:T(8,128)(2,1)} collective-permute-done((bf16[512,1536]{1,0:T(8,128)(2,1)S(1)}, bf16[512,1536]{1,0:T(8,128)(2,1)}, u32[]{:S(2)}, u32[]{:S(2)}) %collective-permute-start.1) | collective-permute-done | bytes 1572896 | tf_op jit(solution)/shard_map/ppermute | solution.py:184
  57.8 3.4 %broadcast_select_fusion.1 = (bf16[512,1536]{1,0:T(8,128)(2,1)}, bf16[512,1536]{1,0:T(8,128)(2,1)}) fusion(bf16[512,1536]{1,0:T(8,128)(2,1)S(1)} %get-tuple-element.39.refs_0_.refs_5_, bf16[512,1536]{1,0:T(8,128)(2,1)} %collective-permute-done.1.refs_4_.refs_9_, pred[]{:T(512)S(6)} %eq.11, pred[]{:T(512)S(6)} %eq.10), kind=kLoop, calls=%fused_computation.20 | loop fusion | flops 1572864 | bytes 6291458 | tf_op jit(solution)/shard_map/jit(_where)/select_n | solution.py:251
  65.0 3.2 %collective-permute-start.6 = (bf16[512,1536]{1,0:T(8,128)(2,1)S(1)}, bf16[512,1536]{1,0:T(8,128)(2,1)}, u32[]{:S(2)}, u32[]{:S(2)}) collective-permute-start(bf16[512,1536]{1,0:T(8,128)(2,1)S(1)} %get-tuple-element.33.refs_0_.refs_5_), channel_id=1, source_target_pairs={{0,8},{2,10},{4,12},{6,14},{8,16},{10,18},{12,20},{14,22},{16,24},... | collective-permute-start | bytes 4718600 | tf_op jit(solution)/shard_map/ppermute | solution.py:184
  68.2 79.9 %collective-permute-done.2 = bf16[12,144,256]{2,1,0:T(8,128)(2,1)} collective-permute-done((bf16[12,144,256]{2,1,0:T(8,128)(2,1)}, bf16[12,144,256]{2,1,0:T(8,128)(2,1)}, u32[]{:S(2)}, u32[]{:S(2)}) %collective-permute-start.2) | collective-permute-done | bytes 884768 | tf_op jit(solution)/shard_map/ppermute | solution.py:187
  149.1 2.7 fusion.4
  151.9 3.3 %broadcast_select_fusion = (bf16[512,1536]{1,0:T(8,128)(2,1)}, bf16[512,1536]{1,0:T(8,128)(2,1)}) fusion(bf16[512,1536]{1,0:T(8,128)(2,1)S(1)} %get-tuple-element.33.refs_0_.refs_5_, bf16[512,1536]{1,0:T(8,128)(2,1)} %collective-permute-done.6.refs_4_.refs_9_, pred[]{:T(512)S(6)} %eq.11, pred[]{:T(512)S(6)} %eq.10), kind=kLoop, calls=%fused_computation.19 | loop fusion | flops 1572864 | bytes 6291458 | tf_op jit(solution)/shard_map/jit(_where)/select_n | solution.py:251
  155.2 3.2 %collective-permute-start.7 = (bf16[12,144,256]{2,1,0:T(8,128)(2,1)S(1)}, bf16[12,144,256]{2,1,0:T(8,128)(2,1)}, u32[]{:S(2)}, u32[]{:S(2)}) collective-permute-start(bf16[12,144,256]{2,1,0:T(8,128)(2,1)S(1)} %pad_maximum_fusion.5), channel_id=1, source_target_pairs={{0,8},{2,10},{4,12},{6,14},{8,16},{10,18},{12,20},{14,22},{16,24},... | collective-permute-start | bytes 2654216 | tf_op jit(solution)/shard_map/ppermute | solution.py:184
  158.4 16.9 %collective-permute-done.7 = bf16[12,144,256]{2,1,0:T(8,128)(2,1)} collective-permute-done((bf16[12,144,256]{2,1,0:T(8,128)(2,1)S(1)}, bf16[12,144,256]{2,1,0:T(8,128)(2,1)}, u32[]{:S(2)}, u32[]{:S(2)}) %collective-permute-start.7) | collective-permute-done | bytes 884768 | tf_op jit(solution)/shard_map/ppermute | solution.py:184
  176.3 2.1 slice.107
  179.7 3.2 %collective-permute-start.8 = (bf16[12,144,256]{2,1,0:T(8,128)(2,1)S(1)}, bf16[12,144,256]{2,1,0:T(8,128)(2,1)}, u32[]{:S(2)}, u32[]{:S(2)}) collective-permute-start(bf16[12,144,256]{2,1,0:T(8,128)(2,1)S(1)} %pad_maximum_fusion.6), channel_id=1, source_target_pairs={{0,8},{2,10},{4,12},{6,14},{8,16},{10,18},{12,20},{14,22},{16,24},... | collective-permute-start | bytes 2654216 | tf_op jit(solution)/shard_map/ppermute | solution.py:184
  185.7 13.2 %collective-permute-done.8 = bf16[12,144,256]{2,1,0:T(8,128)(2,1)} collective-permute-done((bf16[12,144,256]{2,1,0:T(8,128)(2,1)S(1)}, bf16[12,144,256]{2,1,0:T(8,128)(2,1)}, u32[]{:S(2)}, u32[]{:S(2)}) %collective-permute-start.8) | collective-permute-done | bytes 884768 | tf_op jit(solution)/shard_map/ppermute | solution.py:184
  199.8 1.9 fusion.7
  201.9 4.4 %collective-permute-start.9 = (bf16[12,144,256]{2,1,0:T(8,128)(2,1)S(1)}, bf16[12,144,256]{2,1,0:T(8,128)(2,1)S(1)}, u32[]{:S(2)}, u32[]{:S(2)}) collective-permute-start(bf16[12,144,256]{2,1,0:T(8,128)(2,1)S(1)} %pad_maximum_fusion.7), channel_id=1, source_target_pairs={{0,16},{2,18},{4,20},{6,22},{8,24},{10,26},{12,28},{14,30},{1,17},... | collective-permute-start | bytes 2654216 | tf_op jit(solution)/shard_map/ppermute | solution.py:184
  206.4 15.0 %shard_map.133 = bf16[512,768]{1,0:T(8,128)(2,1)S(1)} custom-call(bf16[512,1536]{1,0:T(8,128)(2,1)S(1)} %copy-done, bf16[512,1536]{1,0:T(8,128)(2,1)S(1)} %get-tuple-element.39.refs_0_.refs_5_, bf16[512,1536]{1,0:T(8,128)(2,1)} %collective-permute-done.3.refs_1_.refs_6_, bf16[512,1536]{1,0:T(8,128)(2,1)} %collective-permute-done.4.refs_2_.refs_7_, ...), custom_call_target="tpu_custom_call" | custom-call | flops 4026531840 | bytes 9437184 | tf_op jit(solution)/shard_map/pallas_call | solution.py:146
  221.4 28.3 %collective-permute-done.10.refs_1_.refs_6_ = bf16[512,1536]{1,0:T(8,128)(2,1)} collective-permute-done((bf16[512,1536]{1,0:T(8,128)(2,1)}, bf16[512,1536]{1,0:T(8,128)(2,1)}, u32[]{:S(2)}, u32[]{:S(2)}) %collective-permute-start.10) | collective-permute-done | bytes 1572896 | tf_op jit(solution)/shard_map/ppermute | solution.py:187
  251.2 15.0 %shard_map.134 = bf16[512,768]{1,0:T(8,128)(2,1)S(1)} custom-call(bf16[512,1536]{1,0:T(8,128)(2,1)S(1)} %copy-done, bf16[512,1536]{1,0:T(8,128)(2,1)S(1)} %get-tuple-element.33.refs_0_.refs_5_, bf16[512,1536]{1,0:T(8,128)(2,1)} %collective-permute-done.10.refs_1_.refs_6_, bf16[512,1536]{1,0:T(8,128)(2,1)} %collective-permute-done.11.refs_2_.refs_7_, ...), custom_call_target="tpu_custom_call" | custom-call | flops 4026531840 | bytes 9437184 | tf_op jit(solution)/shard_map/pallas_call | solution.py:146
  267.5 3.0 %fusion.6.incoming_ref = bf16[12,128,256]{2,1,0:T(8,128)(2,1)S(1)} fusion(bf16[12,144,256]{2,1,0:T(8,128)(2,1)S(1)} %collective-permute-done.9, f32[12]{0:T(128)S(1)} %get-tuple-element.50, f32[12]{0:T(128)S(1)} %get-tuple-element.52, f32[12]{0:T(128)S(1)} %get-tuple-element.48, f32[12]{0:T(128)S(1)} %get-tuple-element.46, pred[]{:T(512)S(6)} %ne.13, ...), kind=kLoop, calls=%fused_computation.14 | loop fusion | flops 6291456 | bytes 4718786 | tf_op jit(solution)/shard_map/convert_element_type | solution.py:300
  270.5 11.9 %shard_map.132 = (f32[512,3072]{1,0:T(8,128)}, f32[512,1]{1,0:T(8,128)S(1)}) custom-call(bf16[512,3072]{1,0:T(8,128)(2,1)S(1)} %copy-done.1, bf16[512,3072]{1,0:T(8,128)(2,1)} %gate_ref.1, bf16[512,128]{1,0:T(8,128)(2,1)S(1)} %copy-done.2, bf16[512,128]{1,0:T(8,128)(2,1)S(1)} %copy-done.3, f32[12,1,512]{2,1,0:T(1,128)S(1)} %broadcast_in_dim.38.cum_row_ref, ...), custom_call_target="tpu_custom_call" | custom-call | flops 2013265920 | bytes 12582912 | tf_op jit(solution)/shard_map/pallas_call | solution.py:302
  282.5 6.0 %psum.7 = f32[512]{0:T(512)S(1)} all-reduce(f32[512]{0:T(512)S(1)} %reduce), channel_id=1, replica_groups=mesh['ctx'=16,'head'=2] {'head'}, use_global_device_ids=true, to_apply=%region_0.1 | all-reduce | flops 512 | bytes 4096 | tf_op jit(solution)/shard_map/psum | solution.py:342
  288.5 5.4 %multiply_convert_fusion = bf16[512,3072]{1,0:T(8,128)(2,1)} fusion(f32[512,3072]{1,0:T(8,128)} %get-tuple-element.37, f32[3072]{0:T(1024)S(1)} %copy-done.6, f32[512]{0:T(512)S(1)} %add_rsqrt_fusion), kind=kLoop, calls=%fused_computation | loop fusion | flops 4718592 | bytes 9451520 | tf_op jit(solution)/shard_map/convert_element_type | solution.py:345
  (92 shorter events, 26.7 us)
Async XLA Ops:
  4.3 1.9 copy-start.5
  19.6 20.8 %collective-permute-start = (bf16[12,144,256]{2,1,0:T(8,128)(2,1)}, bf16[12,144,256]{2,1,0:T(8,128)(2,1)}, u32[]{:S(2)}, u32[]{:S(2)}) collective-permute-start(bf16[12,144,256]{2,1,0:T(8,128)(2,1)} %pad_maximum_fusion.3), channel_id=1, source_target_pairs={{0,2},{2,0},{4,6},{6,4},{8,10},{10,8},{12,14},{14,12},{16,18},{18,... | collective-permute-start | bytes 2654216 | tf_op jit(solution)/shard_map/ppermute | solution.py:187
  20.8 36.9 %collective-permute-start.1 = (bf16[512,1536]{1,0:T(8,128)(2,1)S(1)}, bf16[512,1536]{1,0:T(8,128)(2,1)}, u32[]{:S(2)}, u32[]{:S(2)}) collective-permute-start(bf16[512,1536]{1,0:T(8,128)(2,1)S(1)} %get-tuple-element.39.refs_0_.refs_5_), channel_id=1, source_target_pairs={{0,8},{2,10},{4,12},{6,14},{8,16},{10,18},{12,20},{14,22},{16,24},... | collective-permute-start | bytes 4718600 | tf_op jit(solution)/shard_map/ppermute | solution.py:184
  61.1 87.0 %collective-permute-start.3 = (bf16[512,1536]{1,0:T(8,128)(2,1)}, bf16[512,1536]{1,0:T(8,128)(2,1)}, u32[]{:S(2)}, u32[]{:S(2)}) collective-permute-start(bf16[512,1536]{1,0:T(8,128)(2,1)} %get-tuple-element.30), channel_id=1, source_target_pairs={{0,2},{2,0},{4,6},{6,4},{8,10},{10,8},{12,14},{14,12},{16,18},{18,... | collective-permute-start | bytes 4718600 | tf_op jit(solution)/shard_map/ppermute | solution.py:187
  61.4 86.7 %collective-permute-start.4 = (bf16[512,1536]{1,0:T(8,128)(2,1)}, bf16[512,1536]{1,0:T(8,128)(2,1)}, u32[]{:S(2)}, u32[]{:S(2)}) collective-permute-start(bf16[512,1536]{1,0:T(8,128)(2,1)} %get-tuple-element.31), channel_id=1, source_target_pairs={{0,4},{2,6},{4,0},{6,2},{8,12},{10,14},{12,8},{14,10},{16,20},{18,... | collective-permute-start | bytes 4718600 | tf_op jit(solution)/shard_map/ppermute | solution.py:187
  62.6 85.5 %collective-permute-start.5 = (bf16[512,1536]{1,0:T(8,128)(2,1)}, bf16[512,1536]{1,0:T(8,128)(2,1)}, u32[]{:S(2)}, u32[]{:S(2)}) collective-permute-start(bf16[512,1536]{1,0:T(8,128)(2,1)} %get-tuple-element.31), channel_id=1, source_target_pairs={{0,6},{2,4},{4,2},{6,0},{8,14},{10,12},{12,10},{14,8},{16,22},{18,... | collective-permute-start | bytes 4718600 | tf_op jit(solution)/shard_map/ppermute | solution.py:187
  63.8 84.3 %collective-permute-start.2 = (bf16[12,144,256]{2,1,0:T(8,128)(2,1)}, bf16[12,144,256]{2,1,0:T(8,128)(2,1)}, u32[]{:S(2)}, u32[]{:S(2)}) collective-permute-start(bf16[12,144,256]{2,1,0:T(8,128)(2,1)} %pad_maximum_fusion.4), channel_id=1, source_target_pairs={{0,4},{2,6},{4,0},{6,2},{8,12},{10,14},{12,8},{14,10},{16,20},{18,... | collective-permute-start | bytes 2654216 | tf_op jit(solution)/shard_map/ppermute | solution.py:187
  65.0 86.9 %collective-permute-start.6 = (bf16[512,1536]{1,0:T(8,128)(2,1)S(1)}, bf16[512,1536]{1,0:T(8,128)(2,1)}, u32[]{:S(2)}, u32[]{:S(2)}) collective-permute-start(bf16[512,1536]{1,0:T(8,128)(2,1)S(1)} %get-tuple-element.33.refs_0_.refs_5_), channel_id=1, source_target_pairs={{0,8},{2,10},{4,12},{6,14},{8,16},{10,18},{12,20},{14,22},{16,24},... | collective-permute-start | bytes 4718600 | tf_op jit(solution)/shard_map/ppermute | solution.py:184
  155.2 20.1 %collective-permute-start.7 = (bf16[12,144,256]{2,1,0:T(8,128)(2,1)S(1)}, bf16[12,144,256]{2,1,0:T(8,128)(2,1)}, u32[]{:S(2)}, u32[]{:S(2)}) collective-permute-start(bf16[12,144,256]{2,1,0:T(8,128)(2,1)S(1)} %pad_maximum_fusion.5), channel_id=1, source_target_pairs={{0,8},{2,10},{4,12},{6,14},{8,16},{10,18},{12,20},{14,22},{16,24},... | collective-permute-start | bytes 2654216 | tf_op jit(solution)/shard_map/ppermute | solution.py:184
  179.7 19.2 %collective-permute-start.8 = (bf16[12,144,256]{2,1,0:T(8,128)(2,1)S(1)}, bf16[12,144,256]{2,1,0:T(8,128)(2,1)}, u32[]{:S(2)}, u32[]{:S(2)}) collective-permute-start(bf16[12,144,256]{2,1,0:T(8,128)(2,1)S(1)} %pad_maximum_fusion.6), channel_id=1, source_target_pairs={{0,8},{2,10},{4,12},{6,14},{8,16},{10,18},{12,20},{14,22},{16,24},... | collective-permute-start | bytes 2654216 | tf_op jit(solution)/shard_map/ppermute | solution.py:184
  183.0 68.2 %collective-permute-start.11 = (bf16[512,1536]{1,0:T(8,128)(2,1)}, bf16[512,1536]{1,0:T(8,128)(2,1)}, u32[]{:S(2)}, u32[]{:S(2)}) collective-permute-start(bf16[512,1536]{1,0:T(8,128)(2,1)} %get-tuple-element.45), channel_id=1, source_target_pairs={{0,4},{2,6},{4,0},{6,2},{8,12},{10,14},{12,8},{14,10},{16,20},{18,... | collective-permute-start | bytes 4718600 | tf_op jit(solution)/shard_map/ppermute | solution.py:187
  184.3 66.9 %collective-permute-start.12 = (bf16[512,1536]{1,0:T(8,128)(2,1)}, bf16[512,1536]{1,0:T(8,128)(2,1)}, u32[]{:S(2)}, u32[]{:S(2)}) collective-permute-start(bf16[512,1536]{1,0:T(8,128)(2,1)} %get-tuple-element.45), channel_id=1, source_target_pairs={{0,6},{2,4},{4,2},{6,0},{8,14},{10,12},{12,10},{14,8},{16,22},{18,... | collective-permute-start | bytes 4718600 | tf_op jit(solution)/shard_map/ppermute | solution.py:187
  185.4 64.3 %collective-permute-start.10 = (bf16[512,1536]{1,0:T(8,128)(2,1)}, bf16[512,1536]{1,0:T(8,128)(2,1)}, u32[]{:S(2)}, u32[]{:S(2)}) collective-permute-start(bf16[512,1536]{1,0:T(8,128)(2,1)} %get-tuple-element.44), channel_id=1, source_target_pairs={{0,2},{2,0},{4,6},{6,4},{8,10},{10,8},{12,14},{14,12},{16,18},{18,... | collective-permute-start | bytes 4718600 | tf_op jit(solution)/shard_map/ppermute | solution.py:187
  199.8 6.5 %copy-start = (bf16[512,1536]{1,0:T(8,128)(2,1)S(1)}, bf16[512,1536]{1,0:T(8,128)(2,1)}, u32[]{:S(2)}) copy-start(bf16[512,1536]{1,0:T(8,128)(2,1)} %q_ref.3) | copy-start | bytes 4718596
  201.9 65.6 %collective-permute-start.9 = (bf16[12,144,256]{2,1,0:T(8,128)(2,1)S(1)}, bf16[12,144,256]{2,1,0:T(8,128)(2,1)S(1)}, u32[]{:S(2)}, u32[]{:S(2)}) collective-permute-start(bf16[12,144,256]{2,1,0:T(8,128)(2,1)S(1)} %pad_maximum_fusion.7), channel_id=1, source_target_pairs={{0,16},{2,18},{4,20},{6,22},{8,24},{10,26},{12,28},{14,30},{1,17},... | collective-permute-start | bytes 2654216 | tf_op jit(solution)/shard_map/ppermute | solution.py:184
  267.4 3.0 %copy-start.1 = (bf16[512,3072]{1,0:T(8,128)(2,1)S(1)}, bf16[512,3072]{1,0:T(8,128)(2,1)}, u32[]{:S(2)}) copy-start(bf16[512,3072]{1,0:T(8,128)(2,1)} %x_ref.3) | copy-start | bytes 9437188
  267.4 3.0 %copy-start.2 = (bf16[512,128]{1,0:T(8,128)(2,1)S(1)}, bf16[512,128]{1,0:T(8,128)(2,1)}, u32[]{:S(2)}) copy-start(bf16[512,128]{1,0:T(8,128)(2,1)} %write_ref.3) | copy-start | bytes 393220
  267.4 3.0 %copy-start.3 = (bf16[512,128]{1,0:T(8,128)(2,1)S(1)}, bf16[512,128]{1,0:T(8,128)(2,1)}, u32[]{:S(2)}) copy-start(bf16[512,128]{1,0:T(8,128)(2,1)} %read_ref.1) | copy-start | bytes 393220
  267.5 3.0 %copy-start.4 = (f32[12]{0:T(128)S(1)}, f32[12]{0:T(128)}, u32[]{:S(2)}) copy-start(f32[12]{0:T(128)} %param.19) | copy-start | bytes 148
  270.5 18.0 %copy-start.6 = (f32[3072]{0:T(1024)S(1)}, f32[3072]{0:T(1024)}, u32[]{:S(2)}) copy-start(f32[3072]{0:T(1024)} %param.20) | copy-start | bytes 36868

commit v3 on v2

--- a/solution.py
+++ b/solution.py
@@ -241,22 +241,23 @@
     def grown(log):
         return jnp.exp(log)[:, None, None]
 
+    def half_swap(value, bits, forward):
+        return lax.ppermute(
+            value,
+            "ctx",
+            [
+                (source, source ^ bits)
+                for source in range(count)
+                if (source < source ^ bits) == forward
+            ],
+        )
+
+    def both_ways(value, forward):
+        return [half_swap(value, bits, forward) for bits in range(1, group)]
+
     befores = [shift(owns[0], group)]
-    gathered = []
-
-    def exchange(part, before, packed):
-        sent = {}
-        bit = 1
-        while bit < group:
-            sent[bit] = jnp.where(jnp.bitwise_and(mine, bit) == 0, owns[part], before)
-            bit *= 2
-        sent, packed = lax.optimization_barrier((sent, packed))
-        pairs = [owns[part]]
-        for bits in range(1, group):
-            top = 1 << (bits.bit_length() - 1)
-            pairs.append(swap(sent[top], bits))
-        gathered.append(pairs + [before])
-        return packed
+    own_hops = []
+    before_hops = []
 
     prefix = jnp.zeros_like(state)
     prefix_log = jnp.zeros_like(last)
@@ -265,9 +266,11 @@
     packed = pack(total, total_log)
     bit = 1
     while bit < group:
+        if bit == 1:
+            own_hops.append(both_ways(owns[0], True))
         hop = swap(packed, bit)
-        if gathered:
-            hop, gathered[-1] = lax.optimization_barrier((hop, gathered[-1]))
+        if bit > 1:
+            hop, own_hops[0] = lax.optimization_barrier((hop, own_hops[0]))
         other, other_log = unpack(hop)
         later = jnp.bitwise_and(position, bit) != 0
         prefix = jnp.where(later, prefix + grown(prefix_log) * other, prefix)
@@ -277,27 +280,40 @@
         )
         total_log = total_log + other_log
         packed = pack(total, total_log)
-        done = len(gathered)
-        if done < parts:
-            before, packed = lax.optimization_barrier((befores[done], packed))
-            if done + 1 < parts:
-                owns[done + 1], before = lax.optimization_barrier((owns[done + 1], before))
-                befores.append(shift(owns[done + 1], group))
-            packed = exchange(done, before, packed)
+        if bit == 1:
+            befores[0], packed = lax.optimization_barrier((befores[0], packed))
+            if parts > 1:
+                owns[1], packed = lax.optimization_barrier((owns[1], packed))
+                befores.append(shift(owns[1], group))
+            before_hops.append(both_ways(befores[0], False))
+        elif parts > 1 and len(own_hops) == 1:
+            befores[1], owns[1], packed = lax.optimization_barrier((befores[1], owns[1], packed))
+            own_hops.append(both_ways(owns[1], True))
+            before_hops.append(both_ways(befores[1], False))
         bit *= 2
-    while len(gathered) < parts:
-        done = len(gathered)
-        if done + 1 < parts:
-            befores.append(shift(owns[done + 1], group))
-        packed = exchange(done, befores[done], packed)
-    earlier, earlier_log = unpack(shift(packed, group))
+    hop = shift(packed, group)
+    hop, before_hops[0] = lax.optimization_barrier((hop, before_hops[0]))
+    earlier, earlier_log = unpack(hop)
     span = 1
     while span * group < count - group:
-        more, more_log = unpack(shift(pack(earlier, earlier_log), span * group))
+        hop = shift(pack(earlier, earlier_log), span * group)
+        if span == 1 and parts > 1:
+            hop, own_hops[1] = lax.optimization_barrier((hop, own_hops[1]))
+        more, more_log = unpack(hop)
         earlier = earlier + grown(earlier_log) * more
         earlier_log = earlier_log + more_log
         span *= 2
     incoming = (prefix + grown(prefix_log) * earlier).astype(jnp.bfloat16)
+
+    gathered = []
+    for part in range(parts):
+        pairs = [owns[part]]
+        for bits in range(1, group):
+            from_earlier = jnp.bitwise_xor(mine, bits) < mine
+            pairs.append(
+                jnp.where(from_earlier, own_hops[part][bits - 1], before_hops[part][bits - 1])
+            )
+        gathered.append(pairs + [befores[part]])
 
     gated, squares = pl.pallas_call(
         mixer_kernel,

time: 297 us -> 304 us (1.024)
  waiting for transfers between devices: 169 us -> 143 us
  starting transfers between devices: 25 us -> 47.6 us
  other arithmetic: 34.3 us -> 41.6 us
    ppermute x8 -> x2, waiting for transfers between devices: 126 us -> 11.7 us  [per_device(): lax.ppermute(value, 'ctx', [(source, source ^ bits) for source in range(c...]
    ppermute x0 -> x12, waiting for transfers between devices: none -> 90.9 us  [half_swap(): lax.ppermute(value, 'ctx', [(source, source ^ bits) for source in range(c...]
    ppermute x0 -> x12, starting transfers between devices: none -> 29.8 us  [half_swap(): lax.ppermute(value, 'ctx', [(source, source ^ bits) for source in range(c...]
    select_n x2 -> x6, other arithmetic: 6.64 us -> 14.2 us  [per_device(): jnp.where(from_earlier, own_hops[part][bits - 1], before_hops[part][bits...]
    ppermute x8 -> x2, starting transfers between devices: 7.81 us -> 2.44 us  [per_device(): lax.ppermute(value, 'ctx', [(source, source ^ bits) for source in range(c...]
  transfers between devices with their start and end apart: 13 -> 19, of which waited for: 7 -> 10; matrix products, arithmetic and copies ran while one was open for 4% -> 10% of each run, Pallas kernels for 10% -> 10%
where the time goes in v3:
time: 304 us; the launch traced here: 300 us
  waiting for transfers between devices  143 us (47%)
  Pallas kernels  51.8 us (17%)
  starting transfers between devices  47.6 us (16%)
  other arithmetic  41.6 us (14%)
  local copies, waits for them, and re-layouts  8.74 us (3%)
  blocking collectives  5.85 us (2%)
    ppermute x12, waiting for transfers between devices, half_swap(): lax.ppermute(value, 'ctx', [(source, source ^ bits) for source in range(c...  90.9 us
    ppermute x5, waiting for transfers between devices, per_device(): lax.ppermute(value, 'ctx', [(source, source + steps) for source in range(...  40.5 us
    pallas_call x2, Pallas kernels, attend(): pl.pallas_call(functools.partial(attention_kernel, group), grid=(heads,),...  30.3 us
    ppermute x12, starting transfers between devices, half_swap(): lax.ppermute(value, 'ctx', [(source, source ^ bits) for source in range(c...  29.8 us
    ppermute x5, starting transfers between devices, per_device(): lax.ppermute(value, 'ctx', [(source, source + steps) for source in range(...  15.3 us
    select_n x6, other arithmetic, per_device(): jnp.where(from_earlier, own_hops[part][bits - 1], before_hops[part][bits...  14.2 us
    pallas_call x1, Pallas kernels, per_device(): pl.pallas_call(mixer_kernel, grid=(local_heads,), in_specs=[pl.BlockSpec(...  11.9 us
    ppermute x2, waiting for transfers between devices, per_device(): lax.ppermute(value, 'ctx', [(source, source ^ bits) for source in range(c...  11.7 us
  transfers between devices with their start and end apart: 19, of which 10 were waited for; matrix products, arithmetic and copies ran while one was open for 10% of the time, Pallas kernels for 10%

profile of v3, /device:TPU:9, one launch (start us, length us, event | category | flops | bytes accessed | tf_op | source)
XLA Modules:
  0.0 300.0 jit_solution(14369679327341662342)
XLA Ops:
  7.4 9.6 %shard_map.131 = f32[12,128,256]{2,1,0:T(8,128)} custom-call(bf16[512,3072]{1,0:T(8,128)(2,1)} %x_ref.3, bf16[512,128]{1,0:T(8,128)(2,1)} %write_ref.3, f32[512,12]{1,0:T(8,128)} %copy.87.weight_ref), custom_call_target="tpu_custom_call" | custom-call | flops 402653184 | bytes 3145728 | tf_op jit(solution)/shard_map/pallas_call | solution.py:209
  20.8 3.2 %collective-permute-start.1 = (bf16[512,1536]{1,0:T(8,128)(2,1)S(1)}, bf16[512,1536]{1,0:T(8,128)(2,1)}, u32[]{:S(2)}, u32[]{:S(2)}) collective-permute-start(bf16[512,1536]{1,0:T(8,128)(2,1)S(1)} %get-tuple-element.26.refs_0_.refs_5_), channel_id=1, source_target_pairs={{0,8},{2,10},{4,12},{6,14},{8,16},{10,18},{12,20},{14,22},{16,24},... | collective-permute-start | bytes 4718600 | tf_op jit(solution)/shard_map/ppermute | solution.py:184
  24.0 3.4 %collective-permute-start.3 = (bf16[512,1536]{1,0:T(8,128)(2,1)S(1)}, bf16[512,1536]{1,0:T(8,128)(2,1)}, u32[]{:S(2)}, u32[]{:S(2)}) collective-permute-start(bf16[512,1536]{1,0:T(8,128)(2,1)S(1)} %get-tuple-element.26.refs_0_.refs_5_), channel_id=1, source_target_pairs={{0,2},{4,6},{8,10},{12,14},{16,18},{20,22},{24,26},{28,30},{1,3},{... | collective-permute-start | bytes 4718600 | tf_op jit(solution)/shard_map/ppermute | solution.py:245
  27.4 4.3 %collective-permute-start.4 = (bf16[512,1536]{1,0:T(8,128)(2,1)S(1)}, bf16[512,1536]{1,0:T(8,128)(2,1)}, u32[]{:S(2)}, u32[]{:S(2)}) collective-permute-start(bf16[512,1536]{1,0:T(8,128)(2,1)S(1)} %get-tuple-element.26.refs_0_.refs_5_), channel_id=1, source_target_pairs={{0,4},{2,6},{8,12},{10,14},{16,20},{18,22},{24,28},{26,30},{1,5},{... | collective-permute-start | bytes 4718600 | tf_op jit(solution)/shard_map/ppermute | solution.py:245
  34.2 6.2 %collective-permute-done = bf16[12,144,256]{2,1,0:T(8,128)(2,1)} collective-permute-done((bf16[12,144,256]{2,1,0:T(8,128)(2,1)}, bf16[12,144,256]{2,1,0:T(8,128)(2,1)}, u32[]{:S(2)}, u32[]{:S(2)}) %collective-permute-start) | collective-permute-done | bytes 884768 | tf_op jit(solution)/shard_map/ppermute | solution.py:187
  44.6 13.2 %collective-permute-done.1.refs_4_.refs_9_ = bf16[512,1536]{1,0:T(8,128)(2,1)} collective-permute-done((bf16[512,1536]{1,0:T(8,128)(2,1)S(1)}, bf16[512,1536]{1,0:T(8,128)(2,1)}, u32[]{:S(2)}, u32[]{:S(2)}) %collective-permute-start.1) | collective-permute-done | bytes 1572896 | tf_op jit(solution)/shard_map/ppermute | solution.py:184
  60.3 12.8 %collective-permute-done.3 = bf16[512,1536]{1,0:T(8,128)(2,1)} collective-permute-done((bf16[512,1536]{1,0:T(8,128)(2,1)S(1)}, bf16[512,1536]{1,0:T(8,128)(2,1)}, u32[]{:S(2)}, u32[]{:S(2)}) %collective-permute-start.3) | collective-permute-done | bytes 1572896 | tf_op jit(solution)/shard_map/ppermute | solution.py:245
  74.3 22.1 %collective-permute-done.4 = bf16[512,1536]{1,0:T(8,128)(2,1)} collective-permute-done((bf16[512,1536]{1,0:T(8,128)(2,1)S(1)}, bf16[512,1536]{1,0:T(8,128)(2,1)}, u32[]{:S(2)}, u32[]{:S(2)}) %collective-permute-start.4) | collective-permute-done | bytes 1572896 | tf_op jit(solution)/shard_map/ppermute | solution.py:245
  97.7 9.1 %collective-permute-done.5 = bf16[512,1536]{1,0:T(8,128)(2,1)} collective-permute-done((bf16[512,1536]{1,0:T(8,128)(2,1)S(1)}, bf16[512,1536]{1,0:T(8,128)(2,1)}, u32[]{:S(2)}, u32[]{:S(2)}) %collective-permute-start.5) | collective-permute-done | bytes 1572896 | tf_op jit(solution)/shard_map/ppermute | solution.py:245
  106.8 3.2 %collective-permute-start.6 = (bf16[512,1536]{1,0:T(8,128)(2,1)S(1)}, bf16[512,1536]{1,0:T(8,128)(2,1)}, u32[]{:S(2)}, u32[]{:S(2)}) collective-permute-start(bf16[512,1536]{1,0:T(8,128)(2,1)S(1)} %get-tuple-element.34.refs_0_.refs_5_), channel_id=1, source_target_pairs={{0,8},{2,10},{4,12},{6,14},{8,16},{10,18},{12,20},{14,22},{16,24},... | collective-permute-start | bytes 4718600 | tf_op jit(solution)/shard_map/ppermute | solution.py:184
  110.0 5.5 %collective-permute-done.2 = bf16[12,144,256]{2,1,0:T(8,128)(2,1)} collective-permute-done((bf16[12,144,256]{2,1,0:T(8,128)(2,1)}, bf16[12,144,256]{2,1,0:T(8,128)(2,1)}, u32[]{:S(2)}, u32[]{:S(2)}) %collective-permute-start.2) | collective-permute-done | bytes 884768 | tf_op jit(solution)/shard_map/ppermute | solution.py:187
  120.2 23.0 %collective-permute-done.6.refs_4_.refs_9_ = bf16[512,1536]{1,0:T(8,128)(2,1)} collective-permute-done((bf16[512,1536]{1,0:T(8,128)(2,1)S(1)}, bf16[512,1536]{1,0:T(8,128)(2,1)}, u32[]{:S(2)}, u32[]{:S(2)}) %collective-permute-start.6) | collective-permute-done | bytes 1572896 | tf_op jit(solution)/shard_map/ppermute | solution.py:184
  143.1 3.2 %collective-permute-start.7 = (bf16[12,144,256]{2,1,0:T(8,128)(2,1)}, bf16[12,144,256]{2,1,0:T(8,128)(2,1)}, u32[]{:S(2)}, u32[]{:S(2)}) collective-permute-start(bf16[12,144,256]{2,1,0:T(8,128)(2,1)} %pad_maximum_fusion.5), channel_id=1, source_target_pairs={{0,8},{2,10},{4,12},{6,14},{8,16},{10,18},{12,20},{14,22},{16,24},... | collective-permute-start | bytes 2654216 | tf_op jit(solution)/shard_map/ppermute | solution.py:184
  148.8 7.1 %collective-permute-start.13 = (bf16[512,1536]{1,0:T(8,128)(2,1)S(1)}, bf16[512,1536]{1,0:T(8,128)(2,1)}, u32[]{:S(2)}, u32[]{:S(2)}) collective-permute-start(bf16[512,1536]{1,0:T(8,128)(2,1)S(1)} %get-tuple-element.34.refs_0_.refs_5_), channel_id=1, source_target_pairs={{0,4},{2,6},{8,12},{10,14},{16,20},{18,22},{24,28},{26,30},{1,5},{... | collective-permute-start | bytes 4718600 | tf_op jit(solution)/shard_map/ppermute | solution.py:245
  159.7 4.3 %collective-permute-done.7 = bf16[12,144,256]{2,1,0:T(8,128)(2,1)} collective-permute-done((bf16[12,144,256]{2,1,0:T(8,128)(2,1)}, bf16[12,144,256]{2,1,0:T(8,128)(2,1)}, u32[]{:S(2)}, u32[]{:S(2)}) %collective-permute-start.7) | collective-permute-done | bytes 884768 | tf_op jit(solution)/shard_map/ppermute | solution.py:184
  168.4 3.2 %collective-permute-start.11 = (bf16[12,144,256]{2,1,0:T(8,128)(2,1)S(1)}, bf16[12,144,256]{2,1,0:T(8,128)(2,1)S(1)}, u32[]{:S(2)}, u32[]{:S(2)}) collective-permute-start(bf16[12,144,256]{2,1,0:T(8,128)(2,1)S(1)} %pad_maximum_fusion.6), channel_id=1, source_target_pairs={{0,8},{2,10},{4,12},{6,14},{8,16},{10,18},{12,20},{14,22},{16,24},... | collective-permute-start | bytes 2654216 | tf_op jit(solution)/shard_map/ppermute | solution.py:184
  171.6 2.7 broadcast_select_fusion.1.refs_3_.refs_8_
  178.9 15.1 %shard_map.133 = bf16[512,768]{1,0:T(8,128)(2,1)S(1)} custom-call(bf16[512,1536]{1,0:T(8,128)(2,1)S(1)} %copy-done, bf16[512,1536]{1,0:T(8,128)(2,1)S(1)} %get-tuple-element.26.refs_0_.refs_5_, bf16[512,1536]{1,0:T(8,128)(2,1)S(1)} %broadcast_select_fusion.5.refs_1_.refs_6_, bf16[512,1536]{1,0:T(8,128)(2,1)} %broadcast_select_fusion.3.refs_2_.refs_7_, ...), custom_call_target="tpu_custom_call" | custom-call | flops 4026531840 | bytes 9437184 | tf_op jit(solution)/shard_map/pallas_call | solution.py:146
  196.2 24.1 %collective-permute-done.13 = bf16[512,1536]{1,0:T(8,128)(2,1)} collective-permute-done((bf16[512,1536]{1,0:T(8,128)(2,1)S(1)}, bf16[512,1536]{1,0:T(8,128)(2,1)}, u32[]{:S(2)}, u32[]{:S(2)}) %collective-permute-start.13) | collective-permute-done | bytes 1572896 | tf_op jit(solution)/shard_map/ppermute | solution.py:245
  232.8 22.8 %collective-permute-done.16 = bf16[512,1536]{1,0:T(8,128)(2,1)} collective-permute-done((bf16[512,1536]{1,0:T(8,128)(2,1)}, bf16[512,1536]{1,0:T(8,128)(2,1)}, u32[]{:S(2)}, u32[]{:S(2)}) %collective-permute-start.16) | collective-permute-done | bytes 1572896 | tf_op jit(solution)/shard_map/ppermute | solution.py:245
  257.2 15.2 %shard_map.134 = bf16[512,768]{1,0:T(8,128)(2,1)S(1)} custom-call(bf16[512,1536]{1,0:T(8,128)(2,1)S(1)} %copy-done.1, bf16[512,1536]{1,0:T(8,128)(2,1)S(1)} %get-tuple-element.34.refs_0_.refs_5_, bf16[512,1536]{1,0:T(8,128)(2,1)S(1)} %broadcast_select_fusion.4.refs_1_.refs_6_, bf16[512,1536]{1,0:T(8,128)(2,1)} %broadcast_select_fusion.2.refs_2_.refs_7_, ...), custom_call_target="tpu_custom_call" | custom-call | flops 4026531840 | bytes 9437184 | tf_op jit(solution)/shard_map/pallas_call | solution.py:146
  276.7 11.9 %shard_map.132 = (f32[512,3072]{1,0:T(8,128)}, f32[512,1]{1,0:T(8,128)S(1)}) custom-call(bf16[512,3072]{1,0:T(8,128)(2,1)S(1)} %copy-done.4, bf16[512,3072]{1,0:T(8,128)(2,1)} %gate_ref.1, bf16[512,128]{1,0:T(8,128)(2,1)S(1)} %copy-done.5, bf16[512,128]{1,0:T(8,128)(2,1)S(1)} %copy-done.6, f32[12,1,512]{2,1,0:T(1,128)S(1)} %broadcast_in_dim.38.cum_row_ref, ...), custom_call_target="tpu_custom_call" | custom-call | flops 2013265920 | bytes 12582912 | tf_op jit(solution)/shard_map/pallas_call | solution.py:318
  288.7 5.8 %psum.7 = f32[512]{0:T(512)S(1)} all-reduce(f32[512]{0:T(512)S(1)} %reduce), channel_id=1, replica_groups=mesh['ctx'=16,'head'=2] {'head'}, use_global_device_ids=true, to_apply=%region_0.1 | all-reduce | flops 512 | bytes 4096 | tf_op jit(solution)/shard_map/psum | solution.py:358
  294.6 5.4 %multiply_convert_fusion = bf16[512,3072]{1,0:T(8,128)(2,1)} fusion(f32[512,3072]{1,0:T(8,128)} %get-tuple-element.36, f32[3072]{0:T(1024)S(1)} %copy-done.11, f32[512]{0:T(512)S(1)} %add_rsqrt_fusion), kind=kLoop, calls=%fused_computation | loop fusion | flops 4718592 | bytes 9451520 | tf_op jit(solution)/shard_map/convert_element_type | solution.py:361
  (118 shorter events, 62.5 us)
Async XLA Ops:
  19.6 20.8 %collective-permute-start = (bf16[12,144,256]{2,1,0:T(8,128)(2,1)}, bf16[12,144,256]{2,1,0:T(8,128)(2,1)}, u32[]{:S(2)}, u32[]{:S(2)}) collective-permute-start(bf16[12,144,256]{2,1,0:T(8,128)(2,1)} %pad_maximum_fusion.3), channel_id=1, source_target_pairs={{0,2},{2,0},{4,6},{6,4},{8,10},{10,8},{12,14},{14,12},{16,18},{18,... | collective-permute-start | bytes 2654216 | tf_op jit(solution)/shard_map/ppermute | solution.py:187
  20.8 36.9 %collective-permute-start.1 = (bf16[512,1536]{1,0:T(8,128)(2,1)S(1)}, bf16[512,1536]{1,0:T(8,128)(2,1)}, u32[]{:S(2)}, u32[]{:S(2)}) collective-permute-start(bf16[512,1536]{1,0:T(8,128)(2,1)S(1)} %get-tuple-element.26.refs_0_.refs_5_), channel_id=1, source_target_pairs={{0,8},{2,10},{4,12},{6,14},{8,16},{10,18},{12,20},{14,22},{16,24},... | collective-permute-start | bytes 4718600 | tf_op jit(solution)/shard_map/ppermute | solution.py:184
  24.0 49.0 %collective-permute-start.3 = (bf16[512,1536]{1,0:T(8,128)(2,1)S(1)}, bf16[512,1536]{1,0:T(8,128)(2,1)}, u32[]{:S(2)}, u32[]{:S(2)}) collective-permute-start(bf16[512,1536]{1,0:T(8,128)(2,1)S(1)} %get-tuple-element.26.refs_0_.refs_5_), channel_id=1, source_target_pairs={{0,2},{4,6},{8,10},{12,14},{16,18},{20,22},{24,26},{28,30},{1,3},{... | collective-permute-start | bytes 4718600 | tf_op jit(solution)/shard_map/ppermute | solution.py:245
  27.4 69.0 %collective-permute-start.4 = (bf16[512,1536]{1,0:T(8,128)(2,1)S(1)}, bf16[512,1536]{1,0:T(8,128)(2,1)}, u32[]{:S(2)}, u32[]{:S(2)}) collective-permute-start(bf16[512,1536]{1,0:T(8,128)(2,1)S(1)} %get-tuple-element.26.refs_0_.refs_5_), channel_id=1, source_target_pairs={{0,4},{2,6},{8,12},{10,14},{16,20},{18,22},{24,28},{26,30},{1,5},{... | collective-permute-start | bytes 4718600 | tf_op jit(solution)/shard_map/ppermute | solution.py:245
  31.7 75.1 %collective-permute-start.5 = (bf16[512,1536]{1,0:T(8,128)(2,1)S(1)}, bf16[512,1536]{1,0:T(8,128)(2,1)}, u32[]{:S(2)}, u32[]{:S(2)}) collective-permute-start(bf16[512,1536]{1,0:T(8,128)(2,1)S(1)} %get-tuple-element.26.refs_0_.refs_5_), channel_id=1, source_target_pairs={{0,6},{2,4},{8,14},{10,12},{16,22},{18,20},{24,30},{26,28},{1,7},{... | collective-permute-start | bytes 4718600 | tf_op jit(solution)/shard_map/ppermute | solution.py:245
  57.8 57.7 %collective-permute-start.2 = (bf16[12,144,256]{2,1,0:T(8,128)(2,1)}, bf16[12,144,256]{2,1,0:T(8,128)(2,1)}, u32[]{:S(2)}, u32[]{:S(2)}) collective-permute-start(bf16[12,144,256]{2,1,0:T(8,128)(2,1)} %pad_maximum_fusion.4), channel_id=1, source_target_pairs={{0,4},{2,6},{4,0},{6,2},{8,12},{10,14},{12,8},{14,10},{16,20},{18,... | collective-permute-start | bytes 2654216 | tf_op jit(solution)/shard_map/ppermute | solution.py:187
  59.0 89.9 %collective-permute-start.10 = (bf16[512,1536]{1,0:T(8,128)(2,1)}, bf16[512,1536]{1,0:T(8,128)(2,1)}, u32[]{:S(2)}, u32[]{:S(2)}) collective-permute-start(bf16[512,1536]{1,0:T(8,128)(2,1)} %collective-permute-done.1.refs_4_.refs_9_), channel_id=1, source_target_pairs={{4,2},{6,0},{12,10},{14,8},{20,18},{22,16},{28,26},{30,24},{5,3},{... | collective-permute-start | bytes 4718600 | tf_op jit(solution)/shard_map/ppermute | solution.py:245
  73.1 82.9 %collective-permute-start.8 = (bf16[512,1536]{1,0:T(8,128)(2,1)}, bf16[512,1536]{1,0:T(8,128)(2,1)}, u32[]{:S(2)}, u32[]{:S(2)}) collective-permute-start(bf16[512,1536]{1,0:T(8,128)(2,1)} %collective-permute-done.1.refs_4_.refs_9_), channel_id=1, source_target_pairs={{2,0},{6,4},{10,8},{14,12},{18,16},{22,20},{26,24},{30,28},{3,1},{... | collective-permute-start | bytes 4718600 | tf_op jit(solution)/shard_map/ppermute | solution.py:245
  96.4 62.0 %collective-permute-start.9 = (bf16[512,1536]{1,0:T(8,128)(2,1)}, bf16[512,1536]{1,0:T(8,128)(2,1)}, u32[]{:S(2)}, u32[]{:S(2)}) collective-permute-start(bf16[512,1536]{1,0:T(8,128)(2,1)} %collective-permute-done.1.refs_4_.refs_9_), channel_id=1, source_target_pairs={{4,0},{6,2},{12,8},{14,10},{20,16},{22,18},{28,24},{30,26},{5,1},{... | collective-permute-start | bytes 4718600 | tf_op jit(solution)/shard_map/ppermute | solution.py:245
  106.8 36.3 %collective-permute-start.6 = (bf16[512,1536]{1,0:T(8,128)(2,1)S(1)}, bf16[512,1536]{1,0:T(8,128)(2,1)}, u32[]{:S(2)}, u32[]{:S(2)}) collective-permute-start(bf16[512,1536]{1,0:T(8,128)(2,1)S(1)} %get-tuple-element.34.refs_0_.refs_5_), channel_id=1, source_target_pairs={{0,8},{2,10},{4,12},{6,14},{8,16},{10,18},{12,20},{14,22},{16,24},... | collective-permute-start | bytes 4718600 | tf_op jit(solution)/shard_map/ppermute | solution.py:184
  143.1 20.9 %collective-permute-start.7 = (bf16[12,144,256]{2,1,0:T(8,128)(2,1)}, bf16[12,144,256]{2,1,0:T(8,128)(2,1)}, u32[]{:S(2)}, u32[]{:S(2)}) collective-permute-start(bf16[12,144,256]{2,1,0:T(8,128)(2,1)} %pad_maximum_fusion.5), channel_id=1, source_target_pairs={{0,8},{2,10},{4,12},{6,14},{8,16},{10,18},{12,20},{14,22},{16,24},... | collective-permute-start | bytes 2654216 | tf_op jit(solution)/shard_map/ppermute | solution.py:184
  146.4 48.5 %collective-permute-start.12 = (bf16[512,1536]{1,0:T(8,128)(2,1)S(1)}, bf16[512,1536]{1,0:T(8,128)(2,1)}, u32[]{:S(2)}, u32[]{:S(2)}) collective-permute-start(bf16[512,1536]{1,0:T(8,128)(2,1)S(1)} %get-tuple-element.34.refs_0_.refs_5_), channel_id=1, source_target_pairs={{0,2},{4,6},{8,10},{12,14},{16,18},{20,22},{24,26},{28,30},{1,3},{... | collective-permute-start | bytes 4718600 | tf_op jit(solution)/shard_map/ppermute | solution.py:245
  148.8 71.5 %collective-permute-start.13 = (bf16[512,1536]{1,0:T(8,128)(2,1)S(1)}, bf16[512,1536]{1,0:T(8,128)(2,1)}, u32[]{:S(2)}, u32[]{:S(2)}) collective-permute-start(bf16[512,1536]{1,0:T(8,128)(2,1)S(1)} %get-tuple-element.34.refs_0_.refs_5_), channel_id=1, source_target_pairs={{0,4},{2,6},{8,12},{10,14},{16,20},{18,22},{24,28},{26,30},{1,5},{... | collective-permute-start | bytes 4718600 | tf_op jit(solution)/shard_map/ppermute | solution.py:245
  156.0 65.6 %collective-permute-start.14 = (bf16[512,1536]{1,0:T(8,128)(2,1)S(1)}, bf16[512,1536]{1,0:T(8,128)(2,1)}, u32[]{:S(2)}, u32[]{:S(2)}) collective-permute-start(bf16[512,1536]{1,0:T(8,128)(2,1)S(1)} %get-tuple-element.34.refs_0_.refs_5_), channel_id=1, source_target_pairs={{0,6},{2,4},{8,14},{10,12},{16,22},{18,20},{24,30},{26,28},{1,7},{... | collective-permute-start | bytes 4718600 | tf_op jit(solution)/shard_map/ppermute | solution.py:245
  158.4 69.0 %collective-permute-start.18 = (bf16[512,1536]{1,0:T(8,128)(2,1)}, bf16[512,1536]{1,0:T(8,128)(2,1)}, u32[]{:S(2)}, u32[]{:S(2)}) collective-permute-start(bf16[512,1536]{1,0:T(8,128)(2,1)} %collective-permute-done.6.refs_4_.refs_9_), channel_id=1, source_target_pairs={{4,2},{6,0},{12,10},{14,8},{20,18},{22,16},{28,26},{30,24},{5,3},{... | collective-permute-start | bytes 4718600 | tf_op jit(solution)/shard_map/ppermute | solution.py:245
  168.4 53.2 %collective-permute-start.11 = (bf16[12,144,256]{2,1,0:T(8,128)(2,1)S(1)}, bf16[12,144,256]{2,1,0:T(8,128)(2,1)S(1)}, u32[]{:S(2)}, u32[]{:S(2)}) collective-permute-start(bf16[12,144,256]{2,1,0:T(8,128)(2,1)S(1)} %pad_maximum_fusion.6), channel_id=1, source_target_pairs={{0,8},{2,10},{4,12},{6,14},{8,16},{10,18},{12,20},{14,22},{16,24},... | collective-permute-start | bytes 2654216 | tf_op jit(solution)/shard_map/ppermute | solution.py:184
  195.0 35.2 %collective-permute-start.17 = (bf16[512,1536]{1,0:T(8,128)(2,1)}, bf16[512,1536]{1,0:T(8,128)(2,1)}, u32[]{:S(2)}, u32[]{:S(2)}) collective-permute-start(bf16[512,1536]{1,0:T(8,128)(2,1)} %collective-permute-done.6.refs_4_.refs_9_), channel_id=1, source_target_pairs={{4,0},{6,2},{12,8},{14,10},{20,16},{22,18},{28,24},{30,26},{5,1},{... | collective-permute-start | bytes 4718600 | tf_op jit(solution)/shard_map/ppermute | solution.py:245
  220.3 35.3 %collective-permute-start.16 = (bf16[512,1536]{1,0:T(8,128)(2,1)}, bf16[512,1536]{1,0:T(8,128)(2,1)}, u32[]{:S(2)}, u32[]{:S(2)}) collective-permute-start(bf16[512,1536]{1,0:T(8,128)(2,1)} %collective-permute-done.6.refs_4_.refs_9_), channel_id=1, source_target_pairs={{2,0},{6,4},{10,8},{14,12},{18,16},{22,20},{26,24},{30,28},{3,1},{... | collective-permute-start | bytes 4718600 | tf_op jit(solution)/shard_map/ppermute | solution.py:245
  224.8 48.9 %collective-permute-start.15 = (bf16[12,144,256]{2,1,0:T(8,128)(2,1)S(1)}, bf16[12,144,256]{2,1,0:T(8,128)(2,1)S(1)}, u32[]{:S(2)}, u32[]{:S(2)}) collective-permute-start(bf16[12,144,256]{2,1,0:T(8,128)(2,1)S(1)} %pad_maximum_fusion.7), channel_id=1, source_target_pairs={{0,16},{2,18},{4,20},{6,22},{8,24},{10,26},{12,28},{14,30},{1,17},... | collective-permute-start | bytes 2654216 | tf_op jit(solution)/shard_map/ppermute | solution.py:184
  232.8 24.4 %copy-start.1 = (bf16[512,1536]{1,0:T(8,128)(2,1)S(1)}, bf16[512,1536]{1,0:T(8,128)(2,1)}, u32[]{:S(2)}) copy-start(bf16[512,1536]{1,0:T(8,128)(2,1)} %q_ref.3) | copy-start | bytes 4718596
  257.2 15.2 %copy-start.3 = (bf16[512,768]{1,0:T(8,128)(2,1)S(1)}, bf16[512,768]{1,0:T(8,128)(2,1)}, u32[]{:S(2)}) copy-start(bf16[512,768]{1,0:T(8,128)(2,1)} %copy-done.2) | copy-start | bytes 2359300
  273.9 2.8 copy-start.6
  273.9 2.8 copy-start.7
  276.7 17.9 %copy-start.11 = (f32[3072]{0:T(1024)S(1)}, f32[3072]{0:T(1024)}, u32[]{:S(2)}) copy-start(f32[3072]{0:T(1024)} %param.20) | copy-start | bytes 36868
  (7 other events, 12.6 us)

commit v4 on v2

--- a/solution.py
+++ b/solution.py
@@ -152,11 +152,7 @@
         out_specs=pl.BlockSpec(block, lambda h: (0, h)),
         out_shape=jax.ShapeDtypeStruct((rows, heads * HD), jnp.bfloat16),
         compiler_params=pltpu.CompilerParams(vmem_limit_bytes=VMEM_LIMIT),
-        cost_estimate=pl.CostEstimate(
-            flops=4 * heads * rows * rows * (group + 1) * HD,
-            bytes_accessed=2 * heads * rows * HD * (2 * group + 4),
-            transcendentals=heads * rows * rows * (group + 1),
-        ),
+        cost_estimate=pl.CostEstimate(flops=1, bytes_accessed=1, transcendentals=0),
     )(query, *pairs, *pairs)
 
 
@@ -216,11 +212,7 @@
         ],
         out_specs=pl.BlockSpec((1, state_size, P_SIZE), lambda h: (h, 0, 0)),
         out_shape=jax.ShapeDtypeStruct((local_heads, state_size, P_SIZE), jnp.float32),
-        cost_estimate=pl.CostEstimate(
-            flops=2 * local_heads * rows * state_size * P_SIZE,
-            bytes_accessed=2 * local_heads * rows * P_SIZE,
-            transcendentals=0,
-        ),
+        cost_estimate=pl.CostEstimate(flops=1, bytes_accessed=1, transcendentals=0),
     )(space_head_input, state_write_matrix, weights.T)
 
     def pack(value, log):
@@ -290,7 +282,11 @@
         if done + 1 < parts:
             befores.append(shift(owns[done + 1], group))
         packed = exchange(done, befores[done], packed)
-    earlier, earlier_log = unpack(shift(packed, group))
+    hop = shift(packed, group)
+    hop, gathered[-1][1 : group - 1] = lax.optimization_barrier(
+        (hop, gathered[-1][1 : group - 1])
+    )
+    earlier, earlier_log = unpack(hop)
     span = 1
     while span * group < count - group:
         more, more_log = unpack(shift(pack(earlier, earlier_log), span * group))
@@ -323,11 +319,7 @@
         ],
         scratch_shapes=[pltpu.VMEM((rows, rows), jnp.float32)],
         compiler_params=pltpu.CompilerParams(vmem_limit_bytes=VMEM_LIMIT),
-        cost_estimate=pl.CostEstimate(
-            flops=2 * local_heads * rows * (rows + state_size) * P_SIZE,
-            bytes_accessed=8 * local_heads * rows * P_SIZE,
-            transcendentals=local_heads * rows * (rows + P_SIZE),
-        ),
+        cost_estimate=pl.CostEstimate(flops=1, bytes_accessed=1, transcendentals=0),
     )(
         space_head_input,
         mixer_gate_input,
@@ -344,10 +336,11 @@
         gated * lax.rsqrt(squares[:, None] / (SSM_HEADS * P_SIZE) + 1e-05) * output_norm_gain
     ).astype(jnp.bfloat16)
 
-    outs = [
-        attend(attention_query, gathered[part], part * part_heads, part_heads, group)
-        for part in range(parts)
-    ]
+    mixer_out, late_query = lax.optimization_barrier((mixer_out, attention_query))
+    outs = []
+    for part in range(parts):
+        query = attention_query if part + 1 < parts else late_query
+        outs.append(attend(query, gathered[part], part * part_heads, part_heads, group))
     window_out = outs[0] if parts == 1 else jnp.concatenate(outs, axis=1)
     return (mixer_out, window_out)
 

time: 297 us -> 299 us (level)
  waiting for transfers between devices: 169 us -> 178 us
  blocking collectives: 6.02 us -> 2.8 us
    ppermute x5, waiting for transfers between devices: 43.2 us -> 66.8 us  [per_device(): lax.ppermute(value, 'ctx', [(source, source + steps) for source in range(...]
    ppermute x8, waiting for transfers between devices: 126 us -> 111 us  [per_device(): lax.ppermute(value, 'ctx', [(source, source ^ bits) for source in range(c...]
    psum x1, blocking collectives: 6.02 us -> 2.8 us  [per_device(): squares = lax.psum(squares[:, 0], 'head')]
    unnamed x14 -> x32, local copies, waits for them, and re-layouts: 0.31 us -> 3.33 us
  transfers between devices with their start and end apart: 13 -> 13, of which waited for: 7 -> 7; matrix products, arithmetic and copies ran while one was open for 4% -> 5% of each run, Pallas kernels for 10% -> 9%
where the time goes in v4:
time: 299 us; the launch traced here: 297 us
  waiting for transfers between devices  178 us (60%)
  Pallas kernels  51.9 us (17%)
  other arithmetic  31.6 us (11%)
  starting transfers between devices  22.8 us (8%)
  local copies, waits for them, and re-layouts  8.38 us (3%)
    ppermute x8, waiting for transfers between devices, per_device(): lax.ppermute(value, 'ctx', [(source, source ^ bits) for source in range(c...  111 us
    ppermute x5, waiting for transfers between devices, per_device(): lax.ppermute(value, 'ctx', [(source, source + steps) for source in range(...  66.8 us
    pallas_call x2, Pallas kernels, attend(): pl.pallas_call(functools.partial(attention_kernel, group), grid=(heads,),...  30.3 us
    ppermute x5, starting transfers between devices, per_device(): lax.ppermute(value, 'ctx', [(source, source + steps) for source in range(...  17.2 us
    pallas_call x1, Pallas kernels, per_device(): pl.pallas_call(mixer_kernel, grid=(local_heads,), in_specs=[pl.BlockSpec(...  11.9 us
    pallas_call x1, Pallas kernels, per_device(): pl.pallas_call(end_state_kernel, grid=(local_heads,), in_specs=[pl.BlockS...  9.63 us
    convert_element_type x4, other arithmetic, pack(): return jnp.concatenate([value.astype(jnp.bfloat16), extra], axis=1)  7.96 us
    select_n x2, other arithmetic, exchange(): sent[bit] = jnp.where(jnp.bitwise_and(mine, bit) == 0, owns[part], before)  6.03 us
  transfers between devices with their start and end apart: 13, of which 7 were waited for; matrix products, arithmetic and copies ran while one was open for 5% of the time, Pallas kernels for 9%

profile of v4, /device:TPU:9, one launch (start us, length us, event | category | flops | bytes accessed | tf_op | source)
XLA Modules:
  0.0 296.9 jit_solution(13936843422543270811)
XLA Ops:
  7.4 9.6 %shard_map.131 = f32[12,128,256]{2,1,0:T(8,128)} custom-call(bf16[512,3072]{1,0:T(8,128)(2,1)} %x_ref.3, bf16[512,128]{1,0:T(8,128)(2,1)} %write_ref.3, f32[512,12]{1,0:T(8,128)} %copy.87.weight_ref), custom_call_target="tpu_custom_call" | custom-call | flops 1 | bytes 1 | tf_op jit(solution)/shard_map/pallas_call | solution.py:205
  20.8 3.2 %collective-permute-start.1 = (bf16[512,1536]{1,0:T(8,128)(2,1)S(1)}, bf16[512,1536]{1,0:T(8,128)(2,1)}, u32[]{:S(2)}, u32[]{:S(2)}) collective-permute-start(bf16[512,1536]{1,0:T(8,128)(2,1)S(1)} %get-tuple-element.48.refs_0_.refs_5_), channel_id=1, source_target_pairs={{0,8},{2,10},{4,12},{6,14},{8,16},{10,18},{12,20},{14,22},{16,24},... | collective-permute-start | bytes 4718600 | tf_op jit(solution)/shard_map/ppermute | solution.py:180
  24.1 16.4 %collective-permute-done = bf16[12,144,256]{2,1,0:T(8,128)(2,1)} collective-permute-done((bf16[12,144,256]{2,1,0:T(8,128)(2,1)}, bf16[12,144,256]{2,1,0:T(8,128)(2,1)}, u32[]{:S(2)}, u32[]{:S(2)}) %collective-permute-start) | collective-permute-done | bytes 884768 | tf_op jit(solution)/shard_map/ppermute | solution.py:183
  41.5 2.1 fusion.22
  44.6 13.2 %collective-permute-done.1.refs_4_.refs_9_ = bf16[512,1536]{1,0:T(8,128)(2,1)} collective-permute-done((bf16[512,1536]{1,0:T(8,128)(2,1)S(1)}, bf16[512,1536]{1,0:T(8,128)(2,1)}, u32[]{:S(2)}, u32[]{:S(2)}) %collective-permute-start.1) | collective-permute-done | bytes 1572896 | tf_op jit(solution)/shard_map/ppermute | solution.py:180
  57.8 3.3 %broadcast_select_fusion.1 = (bf16[512,1536]{1,0:T(8,128)(2,1)}, bf16[512,1536]{1,0:T(8,128)(2,1)}) fusion(bf16[512,1536]{1,0:T(8,128)(2,1)S(1)} %get-tuple-element.48.refs_0_.refs_5_, bf16[512,1536]{1,0:T(8,128)(2,1)} %collective-permute-done.1.refs_4_.refs_9_, pred[]{:T(512)S(6)} %eq.11, pred[]{:T(512)S(6)} %eq.10), kind=kLoop, calls=%fused_computation.20 | loop fusion | flops 1572864 | bytes 6291458 | tf_op jit(solution)/shard_map/jit(_where)/select_n | solution.py:243
  61.3 2.2 collective-permute-start.5
  64.9 3.2 %collective-permute-start.6 = (bf16[512,1536]{1,0:T(8,128)(2,1)S(1)}, bf16[512,1536]{1,0:T(8,128)(2,1)}, u32[]{:S(2)}, u32[]{:S(2)}) collective-permute-start(bf16[512,1536]{1,0:T(8,128)(2,1)S(1)} %get-tuple-element.38.refs_0_.refs_5_), channel_id=1, source_target_pairs={{0,8},{2,10},{4,12},{6,14},{8,16},{10,18},{12,20},{14,22},{16,24},... | collective-permute-start | bytes 4718600 | tf_op jit(solution)/shard_map/ppermute | solution.py:180
  68.1 81.8 %collective-permute-done.2 = bf16[12,144,256]{2,1,0:T(8,128)(2,1)} collective-permute-done((bf16[12,144,256]{2,1,0:T(8,128)(2,1)}, bf16[12,144,256]{2,1,0:T(8,128)(2,1)}, u32[]{:S(2)}, u32[]{:S(2)}) %collective-permute-start.2) | collective-permute-done | bytes 884768 | tf_op jit(solution)/shard_map/ppermute | solution.py:183
  150.9 2.7 fusion.4
  153.7 2.8 broadcast_select_fusion
  157.0 3.2 %collective-permute-start.7 = (bf16[12,144,256]{2,1,0:T(8,128)(2,1)S(1)}, bf16[12,144,256]{2,1,0:T(8,128)(2,1)S(1)}, u32[]{:S(2)}, u32[]{:S(2)}) collective-permute-start(bf16[12,144,256]{2,1,0:T(8,128)(2,1)S(1)} %pad_maximum_fusion.5), channel_id=1, source_target_pairs={{0,8},{2,10},{4,12},{6,14},{8,16},{10,18},{12,20},{14,22},{16,24},... | collective-permute-start | bytes 2654216 | tf_op jit(solution)/shard_map/ppermute | solution.py:180
  160.2 16.0 %collective-permute-done.7 = bf16[12,144,256]{2,1,0:T(8,128)(2,1)S(1)} collective-permute-done((bf16[12,144,256]{2,1,0:T(8,128)(2,1)S(1)}, bf16[12,144,256]{2,1,0:T(8,128)(2,1)S(1)}, u32[]{:S(2)}, u32[]{:S(2)}) %collective-permute-start.7) | collective-permute-done | bytes 884768 | tf_op jit(solution)/shard_map/ppermute | solution.py:180
  176.2 12.9 %collective-permute-done.8.refs_1_.refs_6_ = bf16[512,1536]{1,0:T(8,128)(2,1)S(1)} collective-permute-done((bf16[512,1536]{1,0:T(8,128)(2,1)S(1)}, bf16[512,1536]{1,0:T(8,128)(2,1)S(1)}, u32[]{:S(2)}, u32[]{:S(2)}) %collective-permute-start.8) | collective-permute-done | bytes 1572896 | tf_op jit(solution)/shard_map/ppermute | solution.py:183
  192.9 3.2 %collective-permute-start.10 = (bf16[12,144,256]{2,1,0:T(8,128)(2,1)S(1)}, bf16[12,144,256]{2,1,0:T(8,128)(2,1)S(1)}, u32[]{:S(2)}, u32[]{:S(2)}) collective-permute-start(bf16[12,144,256]{2,1,0:T(8,128)(2,1)S(1)} %pad_maximum_fusion.6), channel_id=1, source_target_pairs={{0,8},{2,10},{4,12},{6,14},{8,16},{10,18},{12,20},{14,22},{16,24},... | collective-permute-start | bytes 2654216 | tf_op jit(solution)/shard_map/ppermute | solution.py:180
  196.1 15.7 %collective-permute-done.10 = bf16[12,144,256]{2,1,0:T(8,128)(2,1)S(1)} collective-permute-done((bf16[12,144,256]{2,1,0:T(8,128)(2,1)S(1)}, bf16[12,144,256]{2,1,0:T(8,128)(2,1)S(1)}, u32[]{:S(2)}, u32[]{:S(2)}) %collective-permute-start.10) | collective-permute-done | bytes 884768 | tf_op jit(solution)/shard_map/ppermute | solution.py:180
  214.9 4.4 %collective-permute-start.11 = (bf16[12,144,256]{2,1,0:T(8,128)(2,1)S(1)}, bf16[12,144,256]{2,1,0:T(8,128)(2,1)S(1)}, u32[]{:S(2)}, u32[]{:S(2)}) collective-permute-start(bf16[12,144,256]{2,1,0:T(8,128)(2,1)S(1)} %pad_maximum_fusion.7), channel_id=1, source_target_pairs={{0,16},{2,18},{4,20},{6,22},{8,24},{10,26},{12,28},{14,30},{1,17},... | collective-permute-start | bytes 2654216 | tf_op jit(solution)/shard_map/ppermute | solution.py:180
  219.4 15.1 %shard_map.133 = bf16[512,768]{1,0:T(8,128)(2,1)S(1)} custom-call(bf16[512,1536]{1,0:T(8,128)(2,1)S(1)} %copy-done.1, bf16[512,1536]{1,0:T(8,128)(2,1)S(1)} %get-tuple-element.48.refs_0_.refs_5_, bf16[512,1536]{1,0:T(8,128)(2,1)} %collective-permute-done.3.refs_1_.refs_6_, bf16[512,1536]{1,0:T(8,128)(2,1)} %collective-permute-done.4.refs_2_.refs_7_, ...), custom_call_target="tpu_custom_call" | custom-call | flops 1 | bytes 1 | tf_op jit(solution)/shard_map/pallas_call | solution.py:146
  235.4 22.0 %collective-permute-done.11 = bf16[12,144,256]{2,1,0:T(8,128)(2,1)S(1)} collective-permute-done((bf16[12,144,256]{2,1,0:T(8,128)(2,1)S(1)}, bf16[12,144,256]{2,1,0:T(8,128)(2,1)S(1)}, u32[]{:S(2)}, u32[]{:S(2)}) %collective-permute-start.11) | collective-permute-done | bytes 884768 | tf_op jit(solution)/shard_map/ppermute | solution.py:180
  257.4 2.4 fusion.6.incoming_ref
  259.9 11.9 %shard_map.132 = (f32[512,3072]{1,0:T(8,128)}, f32[512,1]{1,0:T(8,128)S(1)}) custom-call(bf16[512,3072]{1,0:T(8,128)(2,1)S(1)} %copy-done, bf16[512,3072]{1,0:T(8,128)(2,1)} %gate_ref.1, bf16[512,128]{1,0:T(8,128)(2,1)S(1)} %copy-done.7, bf16[512,128]{1,0:T(8,128)(2,1)S(1)} %copy-done.8, f32[12,1,512]{2,1,0:T(1,128)S(1)} %broadcast_in_dim.38.cum_row_ref, ...), custom_call_target="tpu_custom_call" | custom-call | flops 1 | bytes 1 | tf_op jit(solution)/shard_map/pallas_call | solution.py:298
  272.0 2.8 psum.7
  274.8 5.6 %multiply_convert_fusion = bf16[512,3072]{1,0:T(8,128)(2,1)} fusion(f32[512,3072]{1,0:T(8,128)} %get-tuple-element.45, f32[3072]{0:T(1024)S(1)} %copy-done.15, f32[512]{0:T(512)S(1)} %add_rsqrt_fusion), kind=kLoop, calls=%fused_computation | loop fusion | flops 4718592 | bytes 9451520 | tf_op jit(solution)/shard_map/convert_element_type | solution.py:337
  280.5 15.2 %shard_map.134 = bf16[512,768]{1,0:T(8,128)(2,1)S(1)} custom-call(bf16[512,1536]{1,0:T(8,128)(2,1)S(1)} %copy-done.2, bf16[512,1536]{1,0:T(8,128)(2,1)S(1)} %get-tuple-element.38.refs_0_.refs_5_, bf16[512,1536]{1,0:T(8,128)(2,1)S(1)} %copy-done.4, bf16[512,1536]{1,0:T(8,128)(2,1)} %collective-permute-done.9.refs_2_.refs_7_, ...), custom_call_target="tpu_custom_call" | custom-call | flops 1 | bytes 1 | tf_op jit(solution)/shard_map/pallas_call | solution.py:146
  (110 shorter events, 25.1 us)
Async XLA Ops:
  19.6 20.8 %collective-permute-start = (bf16[12,144,256]{2,1,0:T(8,128)(2,1)}, bf16[12,144,256]{2,1,0:T(8,128)(2,1)}, u32[]{:S(2)}, u32[]{:S(2)}) collective-permute-start(bf16[12,144,256]{2,1,0:T(8,128)(2,1)} %pad_maximum_fusion.3), channel_id=1, source_target_pairs={{0,2},{2,0},{4,6},{6,4},{8,10},{10,8},{12,14},{14,12},{16,18},{18,... | collective-permute-start | bytes 2654216 | tf_op jit(solution)/shard_map/ppermute | solution.py:183
  20.8 36.9 %collective-permute-start.1 = (bf16[512,1536]{1,0:T(8,128)(2,1)S(1)}, bf16[512,1536]{1,0:T(8,128)(2,1)}, u32[]{:S(2)}, u32[]{:S(2)}) collective-permute-start(bf16[512,1536]{1,0:T(8,128)(2,1)S(1)} %get-tuple-element.48.refs_0_.refs_5_), channel_id=1, source_target_pairs={{0,8},{2,10},{4,12},{6,14},{8,16},{10,18},{12,20},{14,22},{16,24},... | collective-permute-start | bytes 4718600 | tf_op jit(solution)/shard_map/ppermute | solution.py:180
  61.0 88.9 %collective-permute-start.3 = (bf16[512,1536]{1,0:T(8,128)(2,1)}, bf16[512,1536]{1,0:T(8,128)(2,1)}, u32[]{:S(2)}, u32[]{:S(2)}) collective-permute-start(bf16[512,1536]{1,0:T(8,128)(2,1)} %get-tuple-element.35), channel_id=1, source_target_pairs={{0,2},{2,0},{4,6},{6,4},{8,10},{10,8},{12,14},{14,12},{16,18},{18,... | collective-permute-start | bytes 4718600 | tf_op jit(solution)/shard_map/ppermute | solution.py:183
  61.3 88.6 %collective-permute-start.5 = (bf16[512,1536]{1,0:T(8,128)(2,1)}, bf16[512,1536]{1,0:T(8,128)(2,1)}, u32[]{:S(2)}, u32[]{:S(2)}) collective-permute-start(bf16[512,1536]{1,0:T(8,128)(2,1)} %get-tuple-element.36), channel_id=1, source_target_pairs={{0,6},{2,4},{4,2},{6,0},{8,14},{10,12},{12,10},{14,8},{16,22},{18,... | collective-permute-start | bytes 4718600 | tf_op jit(solution)/shard_map/ppermute | solution.py:183
  63.5 86.5 %collective-permute-start.4 = (bf16[512,1536]{1,0:T(8,128)(2,1)}, bf16[512,1536]{1,0:T(8,128)(2,1)}, u32[]{:S(2)}, u32[]{:S(2)}) collective-permute-start(bf16[512,1536]{1,0:T(8,128)(2,1)} %get-tuple-element.36), channel_id=1, source_target_pairs={{0,4},{2,6},{4,0},{6,2},{8,12},{10,14},{12,8},{14,10},{16,20},{18,... | collective-permute-start | bytes 4718600 | tf_op jit(solution)/shard_map/ppermute | solution.py:183
  63.7 86.2 %collective-permute-start.2 = (bf16[12,144,256]{2,1,0:T(8,128)(2,1)}, bf16[12,144,256]{2,1,0:T(8,128)(2,1)}, u32[]{:S(2)}, u32[]{:S(2)}) collective-permute-start(bf16[12,144,256]{2,1,0:T(8,128)(2,1)} %pad_maximum_fusion.4), channel_id=1, source_target_pairs={{0,4},{2,6},{4,0},{6,2},{8,12},{10,14},{12,8},{14,10},{16,20},{18,... | collective-permute-start | bytes 2654216 | tf_op jit(solution)/shard_map/ppermute | solution.py:183
  64.9 88.8 %collective-permute-start.6 = (bf16[512,1536]{1,0:T(8,128)(2,1)S(1)}, bf16[512,1536]{1,0:T(8,128)(2,1)}, u32[]{:S(2)}, u32[]{:S(2)}) collective-permute-start(bf16[512,1536]{1,0:T(8,128)(2,1)S(1)} %get-tuple-element.38.refs_0_.refs_5_), channel_id=1, source_target_pairs={{0,8},{2,10},{4,12},{6,14},{8,16},{10,18},{12,20},{14,22},{16,24},... | collective-permute-start | bytes 4718600 | tf_op jit(solution)/shard_map/ppermute | solution.py:180
  156.5 32.6 %collective-permute-start.8 = (bf16[512,1536]{1,0:T(8,128)(2,1)S(1)}, bf16[512,1536]{1,0:T(8,128)(2,1)S(1)}, u32[]{:S(2)}, u32[]{:S(2)}) collective-permute-start(bf16[512,1536]{1,0:T(8,128)(2,1)S(1)} %get-tuple-element.42), channel_id=1, source_target_pairs={{0,2},{2,0},{4,6},{6,4},{8,10},{10,8},{12,14},{14,12},{16,18},{18,... | collective-permute-start | bytes 4718600 | tf_op jit(solution)/shard_map/ppermute | solution.py:183
  156.8 33.6 %collective-permute-start.9 = (bf16[512,1536]{1,0:T(8,128)(2,1)}, bf16[512,1536]{1,0:T(8,128)(2,1)}, u32[]{:S(2)}, u32[]{:S(2)}) collective-permute-start(bf16[512,1536]{1,0:T(8,128)(2,1)} %get-tuple-element.43), channel_id=1, source_target_pairs={{0,4},{2,6},{4,0},{6,2},{8,12},{10,14},{12,8},{14,10},{16,20},{18,... | collective-permute-start | bytes 4718600 | tf_op jit(solution)/shard_map/ppermute | solution.py:183
  157.0 19.2 %collective-permute-start.7 = (bf16[12,144,256]{2,1,0:T(8,128)(2,1)S(1)}, bf16[12,144,256]{2,1,0:T(8,128)(2,1)S(1)}, u32[]{:S(2)}, u32[]{:S(2)}) collective-permute-start(bf16[12,144,256]{2,1,0:T(8,128)(2,1)S(1)} %pad_maximum_fusion.5), channel_id=1, source_target_pairs={{0,8},{2,10},{4,12},{6,14},{8,16},{10,18},{12,20},{14,22},{16,24},... | collective-permute-start | bytes 2654216 | tf_op jit(solution)/shard_map/ppermute | solution.py:180
  176.2 14.2 %copy-start.10 = (bf16[12,144,256]{2,1,0:T(8,128)(2,1)}, bf16[12,144,256]{2,1,0:T(8,128)(2,1)S(1)}, u32[]{:S(2)}) copy-start(bf16[12,144,256]{2,1,0:T(8,128)(2,1)S(1)} %collective-permute-done.7) | copy-start | bytes 2654212
  192.9 18.9 %collective-permute-start.10 = (bf16[12,144,256]{2,1,0:T(8,128)(2,1)S(1)}, bf16[12,144,256]{2,1,0:T(8,128)(2,1)S(1)}, u32[]{:S(2)}, u32[]{:S(2)}) collective-permute-start(bf16[12,144,256]{2,1,0:T(8,128)(2,1)S(1)} %pad_maximum_fusion.6), channel_id=1, source_target_pairs={{0,8},{2,10},{4,12},{6,14},{8,16},{10,18},{12,20},{14,22},{16,24},... | collective-permute-start | bytes 2654216 | tf_op jit(solution)/shard_map/ppermute | solution.py:180
  214.7 4.7 %copy-start.1 = (bf16[512,1536]{1,0:T(8,128)(2,1)S(1)}, bf16[512,1536]{1,0:T(8,128)(2,1)}, u32[]{:S(2)}) copy-start(bf16[512,1536]{1,0:T(8,128)(2,1)} %q_ref.2) | copy-start | bytes 4718596
  214.9 42.5 %collective-permute-start.11 = (bf16[12,144,256]{2,1,0:T(8,128)(2,1)S(1)}, bf16[12,144,256]{2,1,0:T(8,128)(2,1)S(1)}, u32[]{:S(2)}, u32[]{:S(2)}) collective-permute-start(bf16[12,144,256]{2,1,0:T(8,128)(2,1)S(1)} %pad_maximum_fusion.7), channel_id=1, source_target_pairs={{0,16},{2,18},{4,20},{6,22},{8,24},{10,26},{12,28},{14,30},{1,17},... | collective-permute-start | bytes 2654216 | tf_op jit(solution)/shard_map/ppermute | solution.py:180
  219.3 61.2 %collective-permute-start.12 = (bf16[512,1536]{1,0:T(8,128)(2,1)}, bf16[512,1536]{1,0:T(8,128)(2,1)}, u32[]{:S(2)}, u32[]{:S(2)}) collective-permute-start(bf16[512,1536]{1,0:T(8,128)(2,1)} %get-tuple-element.43), channel_id=1, source_target_pairs={{0,6},{2,4},{4,2},{6,0},{8,14},{10,12},{12,10},{14,8},{16,22},{18,... | collective-permute-start | bytes 4718600 | tf_op jit(solution)/shard_map/ppermute | solution.py:183
  219.4 38.0 %copy-start.11 = (bf16[12,144,256]{2,1,0:T(8,128)(2,1)S(1)}, bf16[12,144,256]{2,1,0:T(8,128)(2,1)}, u32[]{:S(2)}) copy-start(bf16[12,144,256]{2,1,0:T(8,128)(2,1)} %copy-done.10) | copy-start | bytes 2654212
  219.4 38.0 %copy-start.13 = (bf16[12,144,256]{2,1,0:T(8,128)(2,1)S(1)}, bf16[12,144,256]{2,1,0:T(8,128)(2,1)}, u32[]{:S(2)}) copy-start(bf16[12,144,256]{2,1,0:T(8,128)(2,1)} %copy-done.12) | copy-start | bytes 2654212
  257.4 2.5 copy-start.7
  257.4 2.5 copy-start.8
  257.4 2.5 copy-start.9
  259.9 14.9 %copy-start.15 = (f32[3072]{0:T(1024)S(1)}, f32[3072]{0:T(1024)}, u32[]{:S(2)}) copy-start(f32[3072]{0:T(1024)} %param.20) | copy-start | bytes 36868
  274.8 5.6 %copy-start.2 = (bf16[512,1536]{1,0:T(8,128)(2,1)S(1)}, bf16[512,1536]{1,0:T(8,128)(2,1)}, u32[]{:S(2)}) copy-start(bf16[512,1536]{1,0:T(8,128)(2,1)} %q_ref.2) | copy-start | bytes 4718596
  274.8 5.6 %copy-start.4 = (bf16[512,1536]{1,0:T(8,128)(2,1)S(1)}, bf16[512,1536]{1,0:T(8,128)(2,1)}, u32[]{:S(2)}) copy-start(bf16[512,1536]{1,0:T(8,128)(2,1)} %copy-done.3) | copy-start | bytes 4718596
  280.4 15.2 %copy-start.6 = (bf16[512,768]{1,0:T(8,128)(2,1)S(1)}, bf16[512,768]{1,0:T(8,128)(2,1)}, u32[]{:S(2)}) copy-start(bf16[512,768]{1,0:T(8,128)(2,1)} %copy-done.5) | copy-start | bytes 2359300
  (5 other events, 7.4 us)
